TPU v7x, 32 devices: a whole 2x2x4 slice. The times are simulated.
32 devices in a mesh: freq: 2 (over x), sec: 16 (over z, y, core).
Axes of the slice: x: 2, y: 2, z: 4, core: 2. Of those that a mesh axis runs over, the one named last changes fastest.
Arguments:
- layer_trans: bfloat16 [16, 1024, 1024], P('sec'), may hold values from -0.1875 to 0.1875
- layer_refl: bfloat16 [16, 1024, 1024], P('sec'), may hold values from -0.046875 to 0.046875
- source_modes: int32 [256], P('freq'), parts along dimension 0, may hold values from 0 to 1023
Outputs:
- upgoing: bfloat16 [32, 64, 1024], P(('freq', 'sec')), parts along dimension 0
There are 2 independent parts, one for each index of `freq`. A program takes and returns all parts, laid end to end along the dimension named above; an argument that names none is the same for every part. Nothing has to cross between parts.
All inputs are finite; a program needn't handle non-finite values.
Results may differ from a plain program's by a relative error of at most 0.035.
Values may be sent and summed in bfloat16 or wider, within the bound.
A program may use at most 64 MiB of HBM per device.

v0:
```python
import jax
import jax.numpy as jnp
from jax import lax
from jax.sharding import PartitionSpec as P

NB = 4


def from_partner(array, axis, stride):
    return lax.ppermute(array, axis, [(i, i ^ 1 << stride) for i in range(lax.axis_size(axis))])


def from_behind(value, axis, steps):
    count = lax.axis_size(axis)
    first, last = (max(0, -steps), min(count, count - steps))
    return lax.ppermute(value, axis, [(source, source + steps) for source in range(first, last)])


def matmul_nt(left, right):
    return lax.dot_general(
        left, right, (((1,), (1,)), ((), ())), preferred_element_type=jnp.float32
    )


def shards(layer_trans, layer_refl, source_modes):
    position = lax.axis_index("sec")
    section = position // 2
    parity = position % 2
    is_upper = parity == 0
    sections = lax.axis_size("sec") // 2
    trans = layer_trans[0]
    refl = layer_refl[0]
    modes_all = trans.shape[0]
    other_t, other_r = from_partner((trans, refl), "sec", 0)
    upper_t = jnp.where(is_upper, trans, other_t)
    lower_t = jnp.where(is_upper, other_t, trans)
    upper_r = jnp.where(is_upper, refl, other_r)
    lower_r = jnp.where(is_upper, other_r, refl)
    merged_t = jnp.dot(upper_t, lower_t, preferred_element_type=jnp.float32).astype(jnp.bfloat16)
    inner = matmul_nt(lower_r, upper_t).astype(jnp.bfloat16)
    merged_r = (
        upper_r.astype(jnp.float32) + jnp.dot(upper_t, inner, preferred_element_type=jnp.float32)
    ).astype(jnp.bfloat16)
    half_rows = source_modes.shape[0] // 2
    batch_rows = half_rows // NB
    my_modes = lax.dynamic_slice_in_dim(source_modes, parity * half_rows, half_rows, 0)
    columns = jnp.arange(modes_all, dtype=jnp.int32)
    steps = sections + NB - 1

    def down_step(step, carry):
        incoming, echoes = carry
        batch = step - section
        valid = (batch >= 0) & (batch < NB)
        batch_c = jnp.clip(batch, 0, NB - 1)
        batch_modes = lax.dynamic_slice_in_dim(my_modes, batch_c * batch_rows, batch_rows, 0)
        unit_rows = (batch_modes[:, None] == columns[None, :]).astype(jnp.bfloat16)
        current = jnp.where(section == 0, unit_rows, incoming)
        echo = jnp.dot(current, merged_r, preferred_element_type=jnp.float32)
        after = jnp.dot(current, merged_t, preferred_element_type=jnp.float32).astype(jnp.bfloat16)
        previous = lax.dynamic_slice_in_dim(echoes, batch_c * batch_rows, batch_rows, 0)
        echoes = lax.dynamic_update_slice_in_dim(
            echoes, jnp.where(valid, echo, previous), batch_c * batch_rows, 0
        )
        incoming = from_behind(after, "sec", 2)
        return (incoming, echoes)

    start_in = jnp.zeros((batch_rows, modes_all), jnp.bfloat16)
    start_echo = jnp.zeros((half_rows, modes_all), jnp.float32)
    unused_in, echoes = lax.fori_loop(0, steps, down_step, (start_in, start_echo))

    def up_step(step, carry):
        incoming, upgoing = carry
        batch = step - (sections - 1 - section)
        valid = (batch >= 0) & (batch < NB)
        batch_c = jnp.clip(batch, 0, NB - 1)
        echo = lax.dynamic_slice_in_dim(echoes, batch_c * batch_rows, batch_rows, 0)
        value = (echo + matmul_nt(incoming, merged_t)).astype(jnp.bfloat16)
        previous = lax.dynamic_slice_in_dim(upgoing, batch_c * batch_rows, batch_rows, 0)
        upgoing = lax.dynamic_update_slice_in_dim(
            upgoing, jnp.where(valid, value, previous), batch_c * batch_rows, 0
        )
        incoming = from_behind(value, "sec", -2)
        return (incoming, upgoing)

    start_up = jnp.zeros((half_rows, modes_all), jnp.bfloat16)
    unused_up, upgoing = lax.fori_loop(0, steps, up_step, (start_in, start_up))
    return upgoing[None]


def solution(mesh):
    return jax.shard_map(
        shards,
        mesh=mesh,
        in_specs=(P("sec", None, None), P("sec", None, None), P("freq")),
        out_specs=P(("freq", "sec"), None, None),
        check_vma=False,
    )
```

profile of v0, /device:TPU:0, one launch (start us, length us, event | category | flops | bytes accessed | tf_op | source)
XLA Modules:
  0.0 180.7 jit_solution(18380081105397127486)
XLA Ops:
  4.6 5.2 %fusion.16 = bf16[1024,1024]{1,0:T(8,128)(2,1)S(1)} fusion(bf16[1024,1024]{1,0:T(8,128)(2,1)} %collective-permute-done.2, pred[]{:T(512)S(6)} %eq.51, bf16[1,1024,1024]{2,1,0:T(8,128)(2,1)} %param.7), kind=kOutput, calls=%fused_computation.20 | convolution fusion | flops 2150629376 | bytes 6291457 | tf_op jit(solution)/shard_map/dot_general | solution.py:39
  9.8 10.7 %add_convert_fusion = bf16[1024,1024]{1,0:T(8,128)(2,1)} fusion(bf16[1024,1024]{1,0:T(8,128)(2,1)} %collective-permute-done.3, pred[]{:T(512)S(6)} %eq.51, bf16[1024,1024]{1,0:T(8,128)(2,1)} %collective-permute-done.2, bf16[1,1024,1024]{2,1,0:T(8,128)(2,1)} %param.8, bf16[1,1024,1024]{2,1,0:T(8,128)(2,1)} %param.7), kind=kOutput, calls=%fused_computation.10 | convolution fusion | flops 4303355904 | bytes 10485761 | tf_op jit(solution)/shard_map/dot_general | solution.py:42
  20.6 78.4 %while.35 = (s32[]{:T(128)}, bf16[16,1024]{1,0:T(8,128)(2,1)S(1)}, f32[64,1024]{1,0:T(8,128)S(1)}, pred[]{:T(512)}, s32[]{:T(128)}, /*index=5*/s32[64]{0:T(128)S...) while((s32[]{:T(128)}, bf16[16,1024]{1,0:T(8,128)(2,1)S(1)}, ...), condition=%wide.region_1.2_spmd.clone, body=%wide.region_0.1_spmd.clone.sunk | while | flops 67239944 | bytes 4621279 | solution.py:69
  21.1 4.8 %collective-permute-start.1 = (bf16[16,1024]{1,0:T(8,128)(2,1)S(1)}, bf16[16,1024]{1,0:T(8,128)(2,1)S(1)}, u32[]{:S(2)}, u32[]{:S(2)}) collective-permute-start(bf16[16,1024]{1,0:T(8,128)(2,1)S(1)} %convolution_convert_fusion.2), channel_id=1, source_target_pairs={{0,2},{1,3},{2,4},{3,5},{4,6},{5,7},{6,8},{7,9},{8,10},{9,11},{10,... | collective-permute-start | bytes 98312 | tf_op jit(solution)/shard_map/while/body/eval_jaxpr/ppermute | solution.py:16
  41.8 4.6 %collective-permute-start.1 = (bf16[16,1024]{1,0:T(8,128)(2,1)S(1)}, bf16[16,1024]{1,0:T(8,128)(2,1)S(1)}, u32[]{:S(2)}, u32[]{:S(2)}) collective-permute-start(bf16[16,1024]{1,0:T(8,128)(2,1)S(1)} %convolution_convert_fusion.2), channel_id=1, source_target_pairs={{0,2},{1,3},{2,4},{3,5},{4,6},{5,7},{6,8},{7,9},{8,10},{9,11},{10,... | collective-permute-start | bytes 98312 | tf_op jit(solution)/shard_map/while/body/eval_jaxpr/ppermute | solution.py:16
  49.0 4.6 %collective-permute-start.1 = (bf16[16,1024]{1,0:T(8,128)(2,1)S(1)}, bf16[16,1024]{1,0:T(8,128)(2,1)S(1)}, u32[]{:S(2)}, u32[]{:S(2)}) collective-permute-start(bf16[16,1024]{1,0:T(8,128)(2,1)S(1)} %convolution_convert_fusion.2), channel_id=1, source_target_pairs={{0,2},{1,3},{2,4},{3,5},{4,6},{5,7},{6,8},{7,9},{8,10},{9,11},{10,... | collective-permute-start | bytes 98312 | tf_op jit(solution)/shard_map/while/body/eval_jaxpr/ppermute | solution.py:16
  56.2 4.6 %collective-permute-start.1 = (bf16[16,1024]{1,0:T(8,128)(2,1)S(1)}, bf16[16,1024]{1,0:T(8,128)(2,1)S(1)}, u32[]{:S(2)}, u32[]{:S(2)}) collective-permute-start(bf16[16,1024]{1,0:T(8,128)(2,1)S(1)} %convolution_convert_fusion.2), channel_id=1, source_target_pairs={{0,2},{1,3},{2,4},{3,5},{4,6},{5,7},{6,8},{7,9},{8,10},{9,11},{10,... | collective-permute-start | bytes 98312 | tf_op jit(solution)/shard_map/while/body/eval_jaxpr/ppermute | solution.py:16
  63.4 4.6 %collective-permute-start.1 = (bf16[16,1024]{1,0:T(8,128)(2,1)S(1)}, bf16[16,1024]{1,0:T(8,128)(2,1)S(1)}, u32[]{:S(2)}, u32[]{:S(2)}) collective-permute-start(bf16[16,1024]{1,0:T(8,128)(2,1)S(1)} %convolution_convert_fusion.2), channel_id=1, source_target_pairs={{0,2},{1,3},{2,4},{3,5},{4,6},{5,7},{6,8},{7,9},{8,10},{9,11},{10,... | collective-permute-start | bytes 98312 | tf_op jit(solution)/shard_map/while/body/eval_jaxpr/ppermute | solution.py:16
  70.6 4.6 %collective-permute-start.1 = (bf16[16,1024]{1,0:T(8,128)(2,1)S(1)}, bf16[16,1024]{1,0:T(8,128)(2,1)S(1)}, u32[]{:S(2)}, u32[]{:S(2)}) collective-permute-start(bf16[16,1024]{1,0:T(8,128)(2,1)S(1)} %convolution_convert_fusion.2), channel_id=1, source_target_pairs={{0,2},{1,3},{2,4},{3,5},{4,6},{5,7},{6,8},{7,9},{8,10},{9,11},{10,... | collective-permute-start | bytes 98312 | tf_op jit(solution)/shard_map/while/body/eval_jaxpr/ppermute | solution.py:16
  77.8 4.6 %collective-permute-start.1 = (bf16[16,1024]{1,0:T(8,128)(2,1)S(1)}, bf16[16,1024]{1,0:T(8,128)(2,1)S(1)}, u32[]{:S(2)}, u32[]{:S(2)}) collective-permute-start(bf16[16,1024]{1,0:T(8,128)(2,1)S(1)} %convolution_convert_fusion.2), channel_id=1, source_target_pairs={{0,2},{1,3},{2,4},{3,5},{4,6},{5,7},{6,8},{7,9},{8,10},{9,11},{10,... | collective-permute-start | bytes 98312 | tf_op jit(solution)/shard_map/while/body/eval_jaxpr/ppermute | solution.py:16
  85.0 4.6 %collective-permute-start.1 = (bf16[16,1024]{1,0:T(8,128)(2,1)S(1)}, bf16[16,1024]{1,0:T(8,128)(2,1)S(1)}, u32[]{:S(2)}, u32[]{:S(2)}) collective-permute-start(bf16[16,1024]{1,0:T(8,128)(2,1)S(1)} %convolution_convert_fusion.2), channel_id=1, source_target_pairs={{0,2},{1,3},{2,4},{3,5},{4,6},{5,7},{6,8},{7,9},{8,10},{9,11},{10,... | collective-permute-start | bytes 98312 | tf_op jit(solution)/shard_map/while/body/eval_jaxpr/ppermute | solution.py:16
  92.2 4.6 %collective-permute-start.1 = (bf16[16,1024]{1,0:T(8,128)(2,1)S(1)}, bf16[16,1024]{1,0:T(8,128)(2,1)S(1)}, u32[]{:S(2)}, u32[]{:S(2)}) collective-permute-start(bf16[16,1024]{1,0:T(8,128)(2,1)S(1)} %convolution_convert_fusion.2), channel_id=1, source_target_pairs={{0,2},{1,3},{2,4},{3,5},{4,6},{5,7},{6,8},{7,9},{8,10},{9,11},{10,... | collective-permute-start | bytes 98312 | tf_op jit(solution)/shard_map/while/body/eval_jaxpr/ppermute | solution.py:16
  99.0 81.1 %while.34 = (s32[]{:T(128)}, bf16[16,1024]{1,0:T(8,128)(2,1)S(1)}, bf16[64,1024]{1,0:T(8,128)(2,1)S(1)}, s32[]{:T(128)}, f32[64,1024]{1,0:T(8,128)S(1)}, /*index...) while((s32[]{:T(128)}, bf16[16,1024]{1,0:T(8,128)(2,1)S(1)}, ...), condition=%wide.region_3.4_spmd, body=%wide.region_2.3_spmd.sunk | while | flops 33603596 | bytes 2425097 | solution.py:86
  101.0 5.2 %collective-permute-done = bf16[16,1024]{1,0:T(8,128)(2,1)S(1)} collective-permute-done((bf16[16,1024]{1,0:T(8,128)(2,1)S(1)}, bf16[16,1024]{1,0:T(8,128)(2,1)S(1)}, u32[]{:S(2)}, u32[]{:S(2)}) %collective-permute-start) | collective-permute-done | bytes 32800 | tf_op jit(solution)/shard_map/while/body/eval_jaxpr/ppermute | solution.py:16
  108.1 5.6 %collective-permute-done = bf16[16,1024]{1,0:T(8,128)(2,1)S(1)} collective-permute-done((bf16[16,1024]{1,0:T(8,128)(2,1)S(1)}, bf16[16,1024]{1,0:T(8,128)(2,1)S(1)}, u32[]{:S(2)}, u32[]{:S(2)}) %collective-permute-start) | collective-permute-done | bytes 32800 | tf_op jit(solution)/shard_map/while/body/eval_jaxpr/ppermute | solution.py:16
  115.7 5.2 %collective-permute-done = bf16[16,1024]{1,0:T(8,128)(2,1)S(1)} collective-permute-done((bf16[16,1024]{1,0:T(8,128)(2,1)S(1)}, bf16[16,1024]{1,0:T(8,128)(2,1)S(1)}, u32[]{:S(2)}, u32[]{:S(2)}) %collective-permute-start) | collective-permute-done | bytes 32800 | tf_op jit(solution)/shard_map/while/body/eval_jaxpr/ppermute | solution.py:16
  122.8 5.4 %collective-permute-done = bf16[16,1024]{1,0:T(8,128)(2,1)S(1)} collective-permute-done((bf16[16,1024]{1,0:T(8,128)(2,1)S(1)}, bf16[16,1024]{1,0:T(8,128)(2,1)S(1)}, u32[]{:S(2)}, u32[]{:S(2)}) %collective-permute-start) | collective-permute-done | bytes 32800 | tf_op jit(solution)/shard_map/while/body/eval_jaxpr/ppermute | solution.py:16
  130.2 5.4 %collective-permute-done = bf16[16,1024]{1,0:T(8,128)(2,1)S(1)} collective-permute-done((bf16[16,1024]{1,0:T(8,128)(2,1)S(1)}, bf16[16,1024]{1,0:T(8,128)(2,1)S(1)}, u32[]{:S(2)}, u32[]{:S(2)}) %collective-permute-start) | collective-permute-done | bytes 32800 | tf_op jit(solution)/shard_map/while/body/eval_jaxpr/ppermute | solution.py:16
  137.6 5.4 %collective-permute-done = bf16[16,1024]{1,0:T(8,128)(2,1)S(1)} collective-permute-done((bf16[16,1024]{1,0:T(8,128)(2,1)S(1)}, bf16[16,1024]{1,0:T(8,128)(2,1)S(1)}, u32[]{:S(2)}, u32[]{:S(2)}) %collective-permute-start) | collective-permute-done | bytes 32800 | tf_op jit(solution)/shard_map/while/body/eval_jaxpr/ppermute | solution.py:16
  144.9 5.4 %collective-permute-done = bf16[16,1024]{1,0:T(8,128)(2,1)S(1)} collective-permute-done((bf16[16,1024]{1,0:T(8,128)(2,1)S(1)}, bf16[16,1024]{1,0:T(8,128)(2,1)S(1)}, u32[]{:S(2)}, u32[]{:S(2)}) %collective-permute-start) | collective-permute-done | bytes 32800 | tf_op jit(solution)/shard_map/while/body/eval_jaxpr/ppermute | solution.py:16
  152.3 5.7 %collective-permute-done = bf16[16,1024]{1,0:T(8,128)(2,1)S(1)} collective-permute-done((bf16[16,1024]{1,0:T(8,128)(2,1)S(1)}, bf16[16,1024]{1,0:T(8,128)(2,1)S(1)}, u32[]{:S(2)}, u32[]{:S(2)}) %collective-permute-start) | collective-permute-done | bytes 32800 | tf_op jit(solution)/shard_map/while/body/eval_jaxpr/ppermute | solution.py:16
  160.0 5.4 %collective-permute-done = bf16[16,1024]{1,0:T(8,128)(2,1)S(1)} collective-permute-done((bf16[16,1024]{1,0:T(8,128)(2,1)S(1)}, bf16[16,1024]{1,0:T(8,128)(2,1)S(1)}, u32[]{:S(2)}, u32[]{:S(2)}) %collective-permute-start) | collective-permute-done | bytes 32800 | tf_op jit(solution)/shard_map/while/body/eval_jaxpr/ppermute | solution.py:16
  167.3 5.4 %collective-permute-done = bf16[16,1024]{1,0:T(8,128)(2,1)S(1)} collective-permute-done((bf16[16,1024]{1,0:T(8,128)(2,1)S(1)}, bf16[16,1024]{1,0:T(8,128)(2,1)S(1)}, u32[]{:S(2)}, u32[]{:S(2)}) %collective-permute-start) | collective-permute-done | bytes 32800 | tf_op jit(solution)/shard_map/while/body/eval_jaxpr/ppermute | solution.py:16
  174.7 5.4 %collective-permute-done = bf16[16,1024]{1,0:T(8,128)(2,1)S(1)} collective-permute-done((bf16[16,1024]{1,0:T(8,128)(2,1)S(1)}, bf16[16,1024]{1,0:T(8,128)(2,1)S(1)}, u32[]{:S(2)}, u32[]{:S(2)}) %collective-permute-start) | collective-permute-done | bytes 32800 | tf_op jit(solution)/shard_map/while/body/eval_jaxpr/ppermute | solution.py:16
  (90 shorter events, 62.6 us)
Async XLA Ops:
  0.0 4.6 %collective-permute-start.2 = (bf16[1024,1024]{1,0:T(8,128)(2,1)}, bf16[1024,1024]{1,0:T(8,128)(2,1)}, u32[]{:S(2)}, u32[]{:S(2)}) collective-permute-start(bf16[1024,1024]{1,0:T(8,128)(2,1)} %bitcast.33), channel_id=1, source_target_pairs={{0,1},{1,0},{2,3},{3,2},{4,5},{5,4},{6,7},{7,6},{8,9},{9,8},{10,11... | collective-permute-start | bytes 6291464 | tf_op jit(solution)/shard_map/ppermute | solution.py:10
  0.5 9.3 %collective-permute-start.3 = (bf16[1024,1024]{1,0:T(8,128)(2,1)}, bf16[1024,1024]{1,0:T(8,128)(2,1)}, u32[]{:S(2)}, u32[]{:S(2)}) collective-permute-start(bf16[1024,1024]{1,0:T(8,128)(2,1)} %bitcast.34), channel_id=1, source_target_pairs={{0,1},{1,0},{2,3},{3,2},{4,5},{5,4},{6,7},{7,6},{8,9},{9,8},{10,11... | collective-permute-start | bytes 6291464 | tf_op jit(solution)/shard_map/ppermute | solution.py:10
  21.1 6.8 %collective-permute-start.1 = (bf16[16,1024]{1,0:T(8,128)(2,1)S(1)}, bf16[16,1024]{1,0:T(8,128)(2,1)S(1)}, u32[]{:S(2)}, u32[]{:S(2)}) collective-permute-start(bf16[16,1024]{1,0:T(8,128)(2,1)S(1)} %convolution_convert_fusion.2), channel_id=1, source_target_pairs={{0,2},{1,3},{2,4},{3,5},{4,6},{5,7},{6,8},{7,9},{8,10},{9,11},{10,... | collective-permute-start | bytes 98312 | tf_op jit(solution)/shard_map/while/body/eval_jaxpr/ppermute | solution.py:16
  28.4 5.9 %collective-permute-start.1 = (bf16[16,1024]{1,0:T(8,128)(2,1)S(1)}, bf16[16,1024]{1,0:T(8,128)(2,1)S(1)}, u32[]{:S(2)}, u32[]{:S(2)}) collective-permute-start(bf16[16,1024]{1,0:T(8,128)(2,1)S(1)} %convolution_convert_fusion.2), channel_id=1, source_target_pairs={{0,2},{1,3},{2,4},{3,5},{4,6},{5,7},{6,8},{7,9},{8,10},{9,11},{10,... | collective-permute-start | bytes 98312 | tf_op jit(solution)/shard_map/while/body/eval_jaxpr/ppermute | solution.py:16
  34.9 6.4 %collective-permute-start.1 = (bf16[16,1024]{1,0:T(8,128)(2,1)S(1)}, bf16[16,1024]{1,0:T(8,128)(2,1)S(1)}, u32[]{:S(2)}, u32[]{:S(2)}) collective-permute-start(bf16[16,1024]{1,0:T(8,128)(2,1)S(1)} %convolution_convert_fusion.2), channel_id=1, source_target_pairs={{0,2},{1,3},{2,4},{3,5},{4,6},{5,7},{6,8},{7,9},{8,10},{9,11},{10,... | collective-permute-start | bytes 98312 | tf_op jit(solution)/shard_map/while/body/eval_jaxpr/ppermute | solution.py:16
  41.8 6.7 %collective-permute-start.1 = (bf16[16,1024]{1,0:T(8,128)(2,1)S(1)}, bf16[16,1024]{1,0:T(8,128)(2,1)S(1)}, u32[]{:S(2)}, u32[]{:S(2)}) collective-permute-start(bf16[16,1024]{1,0:T(8,128)(2,1)S(1)} %convolution_convert_fusion.2), channel_id=1, source_target_pairs={{0,2},{1,3},{2,4},{3,5},{4,6},{5,7},{6,8},{7,9},{8,10},{9,11},{10,... | collective-permute-start | bytes 98312 | tf_op jit(solution)/shard_map/while/body/eval_jaxpr/ppermute | solution.py:16
  49.0 6.7 %collective-permute-start.1 = (bf16[16,1024]{1,0:T(8,128)(2,1)S(1)}, bf16[16,1024]{1,0:T(8,128)(2,1)S(1)}, u32[]{:S(2)}, u32[]{:S(2)}) collective-permute-start(bf16[16,1024]{1,0:T(8,128)(2,1)S(1)} %convolution_convert_fusion.2), channel_id=1, source_target_pairs={{0,2},{1,3},{2,4},{3,5},{4,6},{5,7},{6,8},{7,9},{8,10},{9,11},{10,... | collective-permute-start | bytes 98312 | tf_op jit(solution)/shard_map/while/body/eval_jaxpr/ppermute | solution.py:16
  56.2 6.7 %collective-permute-start.1 = (bf16[16,1024]{1,0:T(8,128)(2,1)S(1)}, bf16[16,1024]{1,0:T(8,128)(2,1)S(1)}, u32[]{:S(2)}, u32[]{:S(2)}) collective-permute-start(bf16[16,1024]{1,0:T(8,128)(2,1)S(1)} %convolution_convert_fusion.2), channel_id=1, source_target_pairs={{0,2},{1,3},{2,4},{3,5},{4,6},{5,7},{6,8},{7,9},{8,10},{9,11},{10,... | collective-permute-start | bytes 98312 | tf_op jit(solution)/shard_map/while/body/eval_jaxpr/ppermute | solution.py:16
  63.4 6.7 %collective-permute-start.1 = (bf16[16,1024]{1,0:T(8,128)(2,1)S(1)}, bf16[16,1024]{1,0:T(8,128)(2,1)S(1)}, u32[]{:S(2)}, u32[]{:S(2)}) collective-permute-start(bf16[16,1024]{1,0:T(8,128)(2,1)S(1)} %convolution_convert_fusion.2), channel_id=1, source_target_pairs={{0,2},{1,3},{2,4},{3,5},{4,6},{5,7},{6,8},{7,9},{8,10},{9,11},{10,... | collective-permute-start | bytes 98312 | tf_op jit(solution)/shard_map/while/body/eval_jaxpr/ppermute | solution.py:16
  70.6 6.7 %collective-permute-start.1 = (bf16[16,1024]{1,0:T(8,128)(2,1)S(1)}, bf16[16,1024]{1,0:T(8,128)(2,1)S(1)}, u32[]{:S(2)}, u32[]{:S(2)}) collective-permute-start(bf16[16,1024]{1,0:T(8,128)(2,1)S(1)} %convolution_convert_fusion.2), channel_id=1, source_target_pairs={{0,2},{1,3},{2,4},{3,5},{4,6},{5,7},{6,8},{7,9},{8,10},{9,11},{10,... | collective-permute-start | bytes 98312 | tf_op jit(solution)/shard_map/while/body/eval_jaxpr/ppermute | solution.py:16
  77.8 6.7 %collective-permute-start.1 = (bf16[16,1024]{1,0:T(8,128)(2,1)S(1)}, bf16[16,1024]{1,0:T(8,128)(2,1)S(1)}, u32[]{:S(2)}, u32[]{:S(2)}) collective-permute-start(bf16[16,1024]{1,0:T(8,128)(2,1)S(1)} %convolution_convert_fusion.2), channel_id=1, source_target_pairs={{0,2},{1,3},{2,4},{3,5},{4,6},{5,7},{6,8},{7,9},{8,10},{9,11},{10,... | collective-permute-start | bytes 98312 | tf_op jit(solution)/shard_map/while/body/eval_jaxpr/ppermute | solution.py:16
  85.0 6.7 %collective-permute-start.1 = (bf16[16,1024]{1,0:T(8,128)(2,1)S(1)}, bf16[16,1024]{1,0:T(8,128)(2,1)S(1)}, u32[]{:S(2)}, u32[]{:S(2)}) collective-permute-start(bf16[16,1024]{1,0:T(8,128)(2,1)S(1)} %convolution_convert_fusion.2), channel_id=1, source_target_pairs={{0,2},{1,3},{2,4},{3,5},{4,6},{5,7},{6,8},{7,9},{8,10},{9,11},{10,... | collective-permute-start | bytes 98312 | tf_op jit(solution)/shard_map/while/body/eval_jaxpr/ppermute | solution.py:16
  92.2 6.7 %collective-permute-start.1 = (bf16[16,1024]{1,0:T(8,128)(2,1)S(1)}, bf16[16,1024]{1,0:T(8,128)(2,1)S(1)}, u32[]{:S(2)}, u32[]{:S(2)}) collective-permute-start(bf16[16,1024]{1,0:T(8,128)(2,1)S(1)} %convolution_convert_fusion.2), channel_id=1, source_target_pairs={{0,2},{1,3},{2,4},{3,5},{4,6},{5,7},{6,8},{7,9},{8,10},{9,11},{10,... | collective-permute-start | bytes 98312 | tf_op jit(solution)/shard_map/while/body/eval_jaxpr/ppermute | solution.py:16
  99.6 6.5 %collective-permute-start = (bf16[16,1024]{1,0:T(8,128)(2,1)S(1)}, bf16[16,1024]{1,0:T(8,128)(2,1)S(1)}, u32[]{:S(2)}, u32[]{:S(2)}) collective-permute-start(bf16[16,1024]{1,0:T(8,128)(2,1)S(1)} %get-tuple-element.460), channel_id=1, source_target_pairs={{2,0},{3,1},{4,2},{5,3},{6,4},{7,5},{8,6},{9,7},{10,8},{11,9},{12,... | collective-permute-start | bytes 98312 | tf_op jit(solution)/shard_map/while/body/eval_jaxpr/ppermute | solution.py:16
  106.8 6.9 %collective-permute-start = (bf16[16,1024]{1,0:T(8,128)(2,1)S(1)}, bf16[16,1024]{1,0:T(8,128)(2,1)S(1)}, u32[]{:S(2)}, u32[]{:S(2)}) collective-permute-start(bf16[16,1024]{1,0:T(8,128)(2,1)S(1)} %get-tuple-element.460), channel_id=1, source_target_pairs={{2,0},{3,1},{4,2},{5,3},{6,4},{7,5},{8,6},{9,7},{10,8},{11,9},{12,... | collective-permute-start | bytes 98312 | tf_op jit(solution)/shard_map/while/body/eval_jaxpr/ppermute | solution.py:16
  114.4 6.5 %collective-permute-start = (bf16[16,1024]{1,0:T(8,128)(2,1)S(1)}, bf16[16,1024]{1,0:T(8,128)(2,1)S(1)}, u32[]{:S(2)}, u32[]{:S(2)}) collective-permute-start(bf16[16,1024]{1,0:T(8,128)(2,1)S(1)} %get-tuple-element.460), channel_id=1, source_target_pairs={{2,0},{3,1},{4,2},{5,3},{6,4},{7,5},{8,6},{9,7},{10,8},{11,9},{12,... | collective-permute-start | bytes 98312 | tf_op jit(solution)/shard_map/while/body/eval_jaxpr/ppermute | solution.py:16
  121.5 6.7 %collective-permute-start = (bf16[16,1024]{1,0:T(8,128)(2,1)S(1)}, bf16[16,1024]{1,0:T(8,128)(2,1)S(1)}, u32[]{:S(2)}, u32[]{:S(2)}) collective-permute-start(bf16[16,1024]{1,0:T(8,128)(2,1)S(1)} %get-tuple-element.460), channel_id=1, source_target_pairs={{2,0},{3,1},{4,2},{5,3},{6,4},{7,5},{8,6},{9,7},{10,8},{11,9},{12,... | collective-permute-start | bytes 98312 | tf_op jit(solution)/shard_map/while/body/eval_jaxpr/ppermute | solution.py:16
  128.9 6.7 %collective-permute-start = (bf16[16,1024]{1,0:T(8,128)(2,1)S(1)}, bf16[16,1024]{1,0:T(8,128)(2,1)S(1)}, u32[]{:S(2)}, u32[]{:S(2)}) collective-permute-start(bf16[16,1024]{1,0:T(8,128)(2,1)S(1)} %get-tuple-element.460), channel_id=1, source_target_pairs={{2,0},{3,1},{4,2},{5,3},{6,4},{7,5},{8,6},{9,7},{10,8},{11,9},{12,... | collective-permute-start | bytes 98312 | tf_op jit(solution)/shard_map/while/body/eval_jaxpr/ppermute | solution.py:16
  136.2 6.7 %collective-permute-start = (bf16[16,1024]{1,0:T(8,128)(2,1)S(1)}, bf16[16,1024]{1,0:T(8,128)(2,1)S(1)}, u32[]{:S(2)}, u32[]{:S(2)}) collective-permute-start(bf16[16,1024]{1,0:T(8,128)(2,1)S(1)} %get-tuple-element.460), channel_id=1, source_target_pairs={{2,0},{3,1},{4,2},{5,3},{6,4},{7,5},{8,6},{9,7},{10,8},{11,9},{12,... | collective-permute-start | bytes 98312 | tf_op jit(solution)/shard_map/while/body/eval_jaxpr/ppermute | solution.py:16
  143.6 6.8 %collective-permute-start = (bf16[16,1024]{1,0:T(8,128)(2,1)S(1)}, bf16[16,1024]{1,0:T(8,128)(2,1)S(1)}, u32[]{:S(2)}, u32[]{:S(2)}) collective-permute-start(bf16[16,1024]{1,0:T(8,128)(2,1)S(1)} %get-tuple-element.460), channel_id=1, source_target_pairs={{2,0},{3,1},{4,2},{5,3},{6,4},{7,5},{8,6},{9,7},{10,8},{11,9},{12,... | collective-permute-start | bytes 98312 | tf_op jit(solution)/shard_map/while/body/eval_jaxpr/ppermute | solution.py:16
  151.0 7.0 %collective-permute-start = (bf16[16,1024]{1,0:T(8,128)(2,1)S(1)}, bf16[16,1024]{1,0:T(8,128)(2,1)S(1)}, u32[]{:S(2)}, u32[]{:S(2)}) collective-permute-start(bf16[16,1024]{1,0:T(8,128)(2,1)S(1)} %get-tuple-element.460), channel_id=1, source_target_pairs={{2,0},{3,1},{4,2},{5,3},{6,4},{7,5},{8,6},{9,7},{10,8},{11,9},{12,... | collective-permute-start | bytes 98312 | tf_op jit(solution)/shard_map/while/body/eval_jaxpr/ppermute | solution.py:16
  158.6 6.7 %collective-permute-start = (bf16[16,1024]{1,0:T(8,128)(2,1)S(1)}, bf16[16,1024]{1,0:T(8,128)(2,1)S(1)}, u32[]{:S(2)}, u32[]{:S(2)}) collective-permute-start(bf16[16,1024]{1,0:T(8,128)(2,1)S(1)} %get-tuple-element.460), channel_id=1, source_target_pairs={{2,0},{3,1},{4,2},{5,3},{6,4},{7,5},{8,6},{9,7},{10,8},{11,9},{12,... | collective-permute-start | bytes 98312 | tf_op jit(solution)/shard_map/while/body/eval_jaxpr/ppermute | solution.py:16
  166.0 6.7 %collective-permute-start = (bf16[16,1024]{1,0:T(8,128)(2,1)S(1)}, bf16[16,1024]{1,0:T(8,128)(2,1)S(1)}, u32[]{:S(2)}, u32[]{:S(2)}) collective-permute-start(bf16[16,1024]{1,0:T(8,128)(2,1)S(1)} %get-tuple-element.460), channel_id=1, source_target_pairs={{2,0},{3,1},{4,2},{5,3},{6,4},{7,5},{8,6},{9,7},{10,8},{11,9},{12,... | collective-permute-start | bytes 98312 | tf_op jit(solution)/shard_map/while/body/eval_jaxpr/ppermute | solution.py:16
  173.4 6.7 %collective-permute-start = (bf16[16,1024]{1,0:T(8,128)(2,1)S(1)}, bf16[16,1024]{1,0:T(8,128)(2,1)S(1)}, u32[]{:S(2)}, u32[]{:S(2)}) collective-permute-start(bf16[16,1024]{1,0:T(8,128)(2,1)S(1)} %get-tuple-element.460), channel_id=1, source_target_pairs={{2,0},{3,1},{4,2},{5,3},{6,4},{7,5},{8,6},{9,7},{10,8},{11,9},{12,... | collective-permute-start | bytes 98312 | tf_op jit(solution)/shard_map/while/body/eval_jaxpr/ppermute | solution.py:16
  (1 other events, 0.7 us)
where the time goes:
time: 182 us; the launch traced here: 181 us
  starting transfers between devices  64.8 us (36%)
  waiting for transfers between devices  62.9 us (35%)
  matrix products  49.9 us (27%)
  local copies, waits for them, and re-layouts  2.33 us (1%)
    ppermute x22, starting transfers between devices, from_behind(): lax.ppermute(value, axis, [(source, source + steps) for source in range(f...  64.2 us
    ppermute x22, waiting for transfers between devices, from_behind(): lax.ppermute(value, axis, [(source, source + steps) for source in range(f...  59.6 us
    dot_general x11, matrix products, down_step(): echo = jnp.dot(current, merged_r, preferred_element_type=jnp.float32)  22.2 us
    dot_general x1, matrix products, shards(): jnp.dot(upper_t, inner, preferred_element_type=jnp.float32)  10.7 us
    dot_general x11, matrix products, matmul_nt(): lax.dot_general(left, right, (((1,), (1,)), ((), ())), preferred_element_...  7.11 us
    dot_general x1, matrix products, shards(): jnp.dot(upper_t, lower_t, preferred_element_type=jnp.float32)  5.2 us
    dot_general x11, matrix products, down_step(): jnp.dot(current, merged_t, preferred_element_type=jnp.float32)  4.65 us
  transfers between devices with their start and end apart: 24, of which 12 were waited for; matrix products, arithmetic and copies ran while one was open for 16% of the time, Pallas kernels for 0%

commit v1 on v0

v1 whole, which is shorter than its diff:
```python
import functools

import jax
import jax.numpy as jnp
from jax import lax
from jax.experimental import pallas as pl
from jax.experimental.pallas import tpu as pltpu
from jax.sharding import PartitionSpec as P

ROWS = 16
TILE = 256
F32 = jnp.float32
BF16 = jnp.bfloat16
MESH = pl.DeviceIdType.MESH


def nn(left, right):
    return jnp.dot(left, right, preferred_element_type=F32)


def nt(left, right):
    return lax.dot_general(left, right, (((1,), (1,)), ((), ())), preferred_element_type=F32)


def kernel(
    n, modes_ref, trans_ref, refl_ref, out_ref,
    trans, refl, merged, merged_t, inner, merged_r,
    down_in, down_out, up_in, echo,
    local_sem, pair_send, pair_recv, down_send, down_recv, up_send, up_recv,
):
    me = lax.axis_index("sec")
    section = me // 2
    parity = me % 2
    partner = me + 1 - 2 * parity
    sections = n // 2
    is_first = section == 0
    is_last = section == sections - 1
    below = lax.rem(me + 2, n)
    above = lax.rem(me + n - 2, n)
    modes = trans.shape[1]
    half = down_in.shape[0]
    batches = half // ROWS

    loads = []
    for which, (source, target) in enumerate(((trans_ref, trans), (refl_ref, refl))):
        loads.append(pltpu.make_async_copy(source.at[0], target.at[parity], local_sem.at[which]))
    for load in loads:
        load.start()

    barrier = pltpu.get_barrier_semaphore()

    def greet(device):
        pl.semaphore_signal(barrier, inc=1, device_id={"sec": device}, device_id_type=MESH)

    greet(partner)

    @pl.when(jnp.logical_not(is_first))
    def _():
        greet(above)

    @pl.when(jnp.logical_not(is_last))
    def _():
        greet(below)

    @pl.when(jnp.logical_or(is_first, is_last))
    def _():
        pl.semaphore_wait(barrier, 2)

    @pl.when(jnp.logical_not(jnp.logical_or(is_first, is_last)))
    def _():
        pl.semaphore_wait(barrier, 3)

    shares = []
    for which, (source, target) in enumerate(((trans_ref, trans), (refl_ref, refl))):
        shares.append(pltpu.make_async_remote_copy(
            src_ref=source.at[0], dst_ref=target.at[parity],
            send_sem=pair_send.at[which], recv_sem=pair_recv.at[which],
            device_id={"sec": partner}, device_id_type=MESH,
        ))
    for share in shares:
        share.start()

    def batch_rows(batch):
        return pl.ds(pl.multiple_of(batch * ROWS, ROWS), ROWS)

    def down_copy(batch):
        return pltpu.make_async_remote_copy(
            src_ref=down_out.at[batch_rows(batch), :], dst_ref=down_in.at[batch_rows(batch), :],
            send_sem=down_send.at[batch], recv_sem=down_recv.at[batch],
            device_id={"sec": below}, device_id_type=MESH,
        )

    def up_copy(batch):
        return pltpu.make_async_remote_copy(
            src_ref=out_ref.at[0, batch_rows(batch), :], dst_ref=up_in.at[batch_rows(batch), :],
            send_sem=up_send.at[batch], recv_sem=up_recv.at[batch],
            device_id={"sec": above}, device_id_type=MESH,
        )

    def merge_trans():
        def tile(step, carry):
            rows = pl.ds(pl.multiple_of(step * TILE, TILE), TILE)
            block = nn(trans[0, rows, :], trans[1]).astype(BF16)
            merged[rows, :] = block
            merged_t[:, rows] = block.T
            return carry

        lax.fori_loop(0, modes // TILE, tile, 0)

    loads[0].wait()
    shares[0].wait()

    @pl.when(is_first)
    def _():
        count = modes_ref.shape[1]
        row_at = lax.broadcasted_iota(jnp.int32, (count, count), 0)
        col_at = lax.broadcasted_iota(jnp.int32, (count, count), 1)
        spread = jnp.where(row_at == col_at, jnp.broadcast_to(modes_ref[...], (count, count)), 0)
        column = jnp.sum(spread, axis=1, keepdims=True)
        places = lax.broadcasted_iota(jnp.int32, (count, modes), 1)
        unit = (column == places).astype(F32).astype(BF16)
        for which in (0, 1):
            @pl.when(parity == which)
            def _():
                down_in[...] = unit[which * half:(which + 1) * half, :]

        def go(batch, carry):
            rows = batch_rows(batch)
            middle = nn(down_in[rows, :], trans[0]).astype(BF16)
            down_out[rows, :] = nn(middle, trans[1]).astype(BF16)
            down_copy(batch).start()
            return carry

        lax.fori_loop(0, batches, go, 0)
        merge_trans()

    @pl.when(jnp.logical_and(jnp.logical_not(is_first), jnp.logical_not(is_last)))
    def _():
        merge_trans()

        def go(batch, carry):
            rows = batch_rows(batch)
            down_copy(batch).wait_recv()
            down_out[rows, :] = nn(down_in[rows, :], merged[...]).astype(BF16)
            down_copy(batch).start()
            return carry

        lax.fori_loop(0, batches, go, 0)

    loads[1].wait()
    shares[1].wait()

    @pl.when(is_last)
    def _():
        def inner_tile(step, carry):
            rows = pl.ds(pl.multiple_of(step * TILE, TILE), TILE)
            inner[rows, :] = nt(refl[1, rows, :], trans[0]).astype(BF16)
            return carry

        lax.fori_loop(0, modes // TILE, inner_tile, 0)

        def refl_tile(step, carry):
            rows = pl.ds(pl.multiple_of(step * TILE, TILE), TILE)
            merged_r[rows, :] = (
                refl[0, rows, :].astype(F32) + nn(trans[0, rows, :], inner[...])
            ).astype(BF16)
            return carry

        lax.fori_loop(0, modes // TILE, refl_tile, 0)

        def go(batch, carry):
            rows = batch_rows(batch)
            down_copy(batch).wait_recv()
            out_ref[0, rows, :] = nn(down_in[rows, :], merged_r[...]).astype(BF16)
            up_copy(batch).start()
            return carry

        lax.fori_loop(0, batches, go, 0)

    @pl.when(jnp.logical_not(is_last))
    def _():
        field = down_in[...]
        middle = nn(field, trans[0]).astype(BF16)
        lower = nn(middle, refl[1]).astype(BF16)
        echo[...] = nn(field, refl[0]) + nt(lower, trans[0])

        def go(batch, carry):
            rows = batch_rows(batch)
            up_copy(batch).wait_recv()
            out_ref[0, rows, :] = (echo[rows, :] + nn(up_in[rows, :], merged_t[...])).astype(BF16)

            @pl.when(jnp.logical_not(is_first))
            def _():
                up_copy(batch).start()

            return carry

        lax.fori_loop(0, batches, go, 0)

        def sent(batch, carry):
            down_copy(batch).wait_send()
            return carry

        lax.fori_loop(0, batches, sent, 0)

    @pl.when(jnp.logical_not(is_first))
    def _():
        def sent(batch, carry):
            up_copy(batch).wait_send()
            return carry

        lax.fori_loop(0, batches, sent, 0)


def shards(n, layer_trans, layer_refl, source_modes):
    modes = layer_trans.shape[1]
    half = source_modes.shape[0] // 2
    batches = half // ROWS
    square = (modes, modes)
    vmem = pl.BlockSpec(memory_space=pltpu.VMEM)
    anywhere = pl.BlockSpec(memory_space=pl.ANY)
    return pl.pallas_call(
        functools.partial(kernel, n),
        out_shape=jax.ShapeDtypeStruct((1, half, modes), BF16),
        in_specs=[vmem, anywhere, anywhere],
        out_specs=vmem,
        scratch_shapes=[
            pltpu.VMEM((2, *square), BF16),
            pltpu.VMEM((2, *square), BF16),
            pltpu.VMEM(square, BF16),
            pltpu.VMEM(square, BF16),
            pltpu.VMEM(square, BF16),
            pltpu.VMEM(square, BF16),
            pltpu.VMEM((half, modes), BF16),
            pltpu.VMEM((half, modes), BF16),
            pltpu.VMEM((half, modes), BF16),
            pltpu.VMEM((half, modes), F32),
            pltpu.SemaphoreType.DMA((2,)),
            pltpu.SemaphoreType.DMA((2,)),
            pltpu.SemaphoreType.DMA((2,)),
            pltpu.SemaphoreType.DMA((batches,)),
            pltpu.SemaphoreType.DMA((batches,)),
            pltpu.SemaphoreType.DMA((batches,)),
            pltpu.SemaphoreType.DMA((batches,)),
        ],
        compiler_params=pltpu.CompilerParams(
            collective_id=0, has_side_effects=True, vmem_limit_bytes=56 * 1024 * 1024
        ),
    )(source_modes.reshape(1, -1), layer_trans, layer_refl)


def solution(mesh):
    return jax.shard_map(
        functools.partial(shards, mesh.shape["sec"]),
        mesh=mesh,
        in_specs=(P("sec", None, None), P("sec", None, None), P("freq")),
        out_specs=P(("freq", "sec"), None, None),
        check_vma=False,
    )
```

time: 182 us -> 62 us (0.34)
  starting transfers between devices: 64.8 us -> 0 us
  waiting for transfers between devices: 62.9 us -> 0 us
  Pallas kernels: 0 us -> 60.3 us
  matrix products: 49.9 us -> 0 us
    ppermute x24 -> x0, starting transfers between devices: 64.8 us -> none  [the longest x22 64.2 us: from_behind(): lax.ppermute(value, axis, [(source, source + steps) for source in range(f...]
    ppermute x24 -> x0, waiting for transfers between devices: 62.9 us -> none  [the longest x22 59.6 us: from_behind(): lax.ppermute(value, axis, [(source, source + steps) for source in range(f...]
    pallas_call x0 -> x1, Pallas kernels: none -> 60.3 us  [shards(): pl.pallas_call(functools.partial(kernel, n), out_shape=jax.ShapeDtypeStru...]
    dot_general x35 -> x0, matrix products: 49.9 us -> none  [the longest x11 22.2 us: down_step(): echo = jnp.dot(current, merged_r, preferred_element_type=jnp.float32)]
  transfers between devices with their start and end apart: 24 -> 0, of which waited for: 12 -> 0; matrix products, arithmetic and copies ran while one was open for 16% -> 0% of each run, Pallas kernels for 0% -> 0%
where the time goes in v1:
time: 62 us; the launch traced here: 61.9 us
  Pallas kernels  60.3 us (97%)
  local copies, waits for them, and re-layouts  1.57 us (3%)
    pallas_call x1, Pallas kernels, shards(): pl.pallas_call(functools.partial(kernel, n), out_shape=jax.ShapeDtypeStru...  60.3 us
    unnamed x1, local copies, waits for them, and re-layouts  1.57 us

profile of v1, /device:TPU:0, one launch (start us, length us, event | category | flops | bytes accessed | tf_op | source)
XLA Modules:
  0.0 61.9 jit_solution(9302934038223198414)
XLA Ops:
  0.0 60.3 %shard_map.37 = bf16[1,64,1024]{2,1,0:T(8,128)(2,1)} custom-call(s32[1,128]{1,0:T(1,128)} %bitcast.1, bf16[1,1024,1024]{2,1,0:T(8,128)(2,1)} %trans_ref.1, bf16[1,1024,1024]{2,1,0:T(8,128)(2,1)} %refl_ref.1), custom_call_target="tpu_custom_call" | custom-call | tf_op jit(solution)/shard_map/pallas_call | solution.py:222
  60.3 1.6 %copy.5 = bf16[1,64,1024]{2,1,0:T(8,128)(2,1)} copy(bf16[1,64,1024]{2,1,0:T(8,128)(2,1)} %shard_map.37) | data formatting | bytes 262144

commit v2 on v0

v2 whole, which is shorter than its diff:
```python
import functools

import jax
import jax.numpy as jnp
from jax import lax
from jax.experimental import pallas as pl
from jax.experimental.pallas import tpu as pltpu
from jax.sharding import PartitionSpec as P

ROWS = 32
TILE = 256
F32 = jnp.float32
BF16 = jnp.bfloat16
MESH = pl.DeviceIdType.MESH


def nn(left, right):
    return jnp.dot(left, right, preferred_element_type=F32)


def each(count, body):
    def step(index, carry):
        body(index)
        return carry

    lax.fori_loop(0, count, step, 0)


def kernel(
    n, modes_ref, trans_ref, refl_ref, out_ref,
    upper_t, lower_t, upper_r, lower_r, merged, merged_t, inner,
    down_in, down_out, up_in, up_out, half_in, echo,
    local_sem, tile_send, tile_recv, pair_send, pair_recv, echo_sem,
    down_send, down_recv, pass_send, up_send, up_recv, half_send, half_recv,
):
    me = lax.axis_index("sec")
    section = me // 2
    parity = me % 2
    partner = me + 1 - 2 * parity
    sections = n // 2
    is_first = section == 0
    is_last = section == sections - 1
    not_first = jnp.logical_not(is_first)
    not_last = jnp.logical_not(is_last)
    on_zero = parity == 0
    on_one = parity == 1
    is_chain = jnp.logical_and(on_one, not_last)
    is_echo = jnp.logical_and(on_zero, not_last)
    is_turn = jnp.logical_and(on_zero, is_last)
    below = lax.rem(jnp.where(section == sections - 2, me + 1, me + 2), n)
    above = lax.rem(me + n - 1 - parity, n)
    modes = upper_t.shape[0]
    tiles = modes // TILE
    batches = down_in.shape[0] // ROWS
    half_batches = batches // 2
    half = half_in.shape[0]

    def tile_rows(tile):
        return pl.ds(pl.multiple_of(tile * TILE, TILE), TILE)

    def batch_rows(batch):
        return pl.ds(pl.multiple_of(batch * ROWS, ROWS), ROWS)

    def remote(source, target, send_sem, recv_sem, device):
        return pltpu.make_async_remote_copy(
            src_ref=source, dst_ref=target, send_sem=send_sem, recv_sem=recv_sem,
            device_id={"sec": device}, device_id_type=MESH,
        )

    load_t0 = pltpu.make_async_copy(trans_ref.at[0], upper_t, local_sem.at[0])
    load_t1 = pltpu.make_async_copy(trans_ref.at[0], lower_t, local_sem.at[0])
    load_r0 = pltpu.make_async_copy(refl_ref.at[0], upper_r, local_sem.at[1])

    @pl.when(on_zero)
    def _():
        load_t0.start()
        load_r0.start()

    @pl.when(on_one)
    def _():
        load_t1.start()

    barrier = pltpu.get_barrier_semaphore()

    def greet(device):
        pl.semaphore_signal(barrier, inc=1, device_id={"sec": device}, device_id_type=MESH)

    has_below = is_chain
    has_above = jnp.logical_or(is_turn, jnp.logical_and(is_chain, not_first))
    greet(partner)

    @pl.when(has_above)
    def _():
        greet(above)

    @pl.when(has_below)
    def _():
        greet(below)

    peers = 1 + has_above.astype(jnp.int32) + has_below.astype(jnp.int32)
    pl.semaphore_wait(barrier, peers)

    def tile_copy(tile):
        return remote(
            trans_ref.at[0, tile_rows(tile), :], upper_t.at[tile_rows(tile), :],
            tile_send.at[tile], tile_recv.at[tile], partner,
        )

    share_r = remote(refl_ref.at[0], lower_r, pair_send, pair_recv, partner)
    give_echo = remote(echo, echo, echo_sem.at[0], echo_sem.at[1], partner)

    def down_copy(batch):
        return remote(
            down_out.at[batch_rows(batch), :], down_in.at[batch_rows(batch), :],
            down_send.at[batch], down_recv.at[batch], below,
        )

    def middle_copy(batch):
        return remote(
            down_out.at[batch_rows(batch), :], down_in.at[batch_rows(batch), :],
            down_send.at[batch], down_recv.at[batch], partner,
        )

    def pass_copy(batch):
        return remote(
            down_in.at[batch_rows(batch), :], down_in.at[batch_rows(batch), :],
            pass_send.at[batch], down_recv.at[batch], partner,
        )

    def up_copy(batch):
        return remote(
            up_out.at[batch_rows(batch), :], up_in.at[batch_rows(batch), :],
            up_send.at[batch], up_recv.at[batch], above,
        )

    def half_copy(place):
        batch = (1 - parity) * half_batches + place
        return remote(
            up_out.at[batch_rows(batch), :], half_in.at[batch_rows(place), :],
            half_send.at[place], half_recv.at[place], partner,
        )

    def unit_rows():
        count = modes_ref.shape[1]
        row_at = lax.broadcasted_iota(jnp.int32, (count, count), 0)
        col_at = lax.broadcasted_iota(jnp.int32, (count, count), 1)
        spread = jnp.where(row_at == col_at, jnp.broadcast_to(modes_ref[...], (count, count)), 0)
        column = jnp.sum(spread, axis=1, keepdims=True)
        places = lax.broadcasted_iota(jnp.int32, (count, modes), 1)
        return (column == places).astype(F32).astype(BF16)

    def own_half():
        for which in (0, 1):
            @pl.when(parity == which)
            def _():
                out_ref[0] = up_out[which * half:(which + 1) * half, :]

    @pl.when(on_zero)
    def _():
        @pl.when(is_first)
        def _():
            down_in[...] = unit_rows()
            load_t0.wait()

            def go(batch):
                rows = batch_rows(batch)
                down_out[rows, :] = nn(down_in[rows, :], upper_t[...]).astype(BF16)
                middle_copy(batch).start()

            each(batches, go)

        each(tiles, lambda tile: tile_copy(tile).start())

        @pl.when(not_first)
        def _():
            load_t0.wait()

        def turn_tile(tile):
            merged_t[:, tile_rows(tile)] = upper_t[tile_rows(tile), :].T

        each(tiles, turn_tile)
        load_r0.wait()
        share_r.wait_recv()

        @pl.when(is_last)
        def _():
            def inner_tile(tile):
                rows = tile_rows(tile)
                inner[rows, :] = nn(lower_r[rows, :], merged_t[...]).astype(BF16)

            each(tiles, inner_tile)

            def refl_tile(tile):
                rows = tile_rows(tile)
                merged[rows, :] = (
                    upper_r[rows, :].astype(F32) + nn(upper_t[rows, :], inner[...])
                ).astype(BF16)

            each(tiles, refl_tile)

            def go(batch):
                rows = batch_rows(batch)
                down_copy(batch).wait_recv()
                up_out[rows, :] = nn(down_in[rows, :], merged[...]).astype(BF16)
                up_copy(batch).start()

            each(batches, go)
            each(half_batches, lambda place: half_copy(place).start())
            own_half()
            each(batches, lambda batch: up_copy(batch).wait_send())
            each(half_batches, lambda place: half_copy(place).wait_send())

        @pl.when(not_last)
        def _():
            @pl.when(not_first)
            def _():
                each(batches, lambda batch: pass_copy(batch).wait_recv())

            field = down_in[...]
            middle = nn(field, upper_t[...]).astype(BF16)
            lower = nn(middle, lower_r[...]).astype(BF16)
            echo[...] = nn(field, upper_r[...]) + nn(lower, merged_t[...])
            give_echo.start()

            @pl.when(is_first)
            def _():
                each(batches, lambda batch: middle_copy(batch).wait_send())

            each(half_batches, lambda place: half_copy(place).wait_recv())
            out_ref[0] = half_in[...]
            give_echo.wait_send()

        each(tiles, lambda tile: tile_copy(tile).wait_send())

    @pl.when(on_one)
    def _():
        share_r.start()
        load_t1.wait()

        @pl.when(is_first)
        def _():
            def go(batch):
                rows = batch_rows(batch)
                middle_copy(batch).wait_recv()
                down_out[rows, :] = nn(down_in[rows, :], lower_t[...]).astype(BF16)
                down_copy(batch).start()

            each(batches, go)

        @pl.when(section == 1)
        def _():
            each(tiles, lambda tile: tile_copy(tile).wait_recv())

        @pl.when(jnp.logical_and(section == 1, not_last))
        def _():
            def go(batch):
                rows = batch_rows(batch)
                down_copy(batch).wait_recv()
                middle = nn(down_in[rows, :], upper_t[...]).astype(BF16)
                down_out[rows, :] = nn(middle, lower_t[...]).astype(BF16)
                down_copy(batch).start()
                pass_copy(batch).start()

            each(batches, go)

        def merge_tile(tile):
            rows = tile_rows(tile)

            @pl.when(section != 1)
            def _():
                tile_copy(tile).wait_recv()

            block = nn(upper_t[rows, :], lower_t[...]).astype(BF16)
            merged[rows, :] = block
            merged_t[:, rows] = block.T

        each(tiles, merge_tile)

        @pl.when(jnp.logical_and(section > 1, not_last))
        def _():
            def go(batch):
                rows = batch_rows(batch)
                down_copy(batch).wait_recv()
                down_out[rows, :] = nn(down_in[rows, :], merged[...]).astype(BF16)
                down_copy(batch).start()
                pass_copy(batch).start()

            each(batches, go)

        @pl.when(not_last)
        def _():
            give_echo.wait_recv()

            def go(batch):
                rows = batch_rows(batch)
                up_copy(batch).wait_recv()
                up_out[rows, :] = (echo[rows, :] + nn(up_in[rows, :], merged_t[...])).astype(BF16)

                @pl.when(not_first)
                def _():
                    up_copy(batch).start()

                @pl.when(batch < half_batches)
                def _():
                    half_copy(batch).start()

            each(batches, go)
            own_half()
            each(batches, lambda batch: down_copy(batch).wait_send())
            each(half_batches, lambda place: half_copy(place).wait_send())

            @pl.when(not_first)
            def _():
                each(batches, lambda batch: up_copy(batch).wait_send())
                each(batches, lambda batch: pass_copy(batch).wait_send())

        @pl.when(is_last)
        def _():
            each(half_batches, lambda place: half_copy(place).wait_recv())
            out_ref[0] = half_in[...]

        share_r.wait_send()


def shards(n, layer_trans, layer_refl, source_modes):
    modes = layer_trans.shape[1]
    count = source_modes.shape[0]
    half = count // 2
    batches = count // ROWS
    square = (modes, modes)
    vmem = pl.BlockSpec(memory_space=pltpu.VMEM)
    anywhere = pl.BlockSpec(memory_space=pl.ANY)
    tiles = pltpu.SemaphoreType.DMA((modes // TILE,))
    per_batch = pltpu.SemaphoreType.DMA((batches,))
    per_half = pltpu.SemaphoreType.DMA((batches // 2,))
    return pl.pallas_call(
        functools.partial(kernel, n),
        out_shape=jax.ShapeDtypeStruct((1, half, modes), BF16),
        in_specs=[vmem, anywhere, anywhere],
        out_specs=vmem,
        scratch_shapes=[pltpu.VMEM(square, BF16)] * 7 + [
            pltpu.VMEM((count, modes), BF16),
            pltpu.VMEM((count, modes), BF16),
            pltpu.VMEM((count, modes), BF16),
            pltpu.VMEM((count, modes), BF16),
            pltpu.VMEM((half, modes), BF16),
            pltpu.VMEM((count, modes), F32),
            pltpu.SemaphoreType.DMA((2,)),
            tiles,
            tiles,
            pltpu.SemaphoreType.DMA,
            pltpu.SemaphoreType.DMA,
            pltpu.SemaphoreType.DMA((2,)),
            per_batch,
            per_batch,
            per_batch,
            per_batch,
            per_batch,
            per_half,
            per_half,
        ],
        compiler_params=pltpu.CompilerParams(
            collective_id=0, has_side_effects=True, vmem_limit_bytes=56 * 1024 * 1024
        ),
    )(source_modes.reshape(1, -1), layer_trans, layer_refl)


def solution(mesh):
    return jax.shard_map(
        functools.partial(shards, mesh.shape["sec"]),
        mesh=mesh,
        in_specs=(P("sec", None, None), P("sec", None, None), P("freq")),
        out_specs=P(("freq", "sec"), None, None),
        check_vma=False,
    )
```

time: 182 us -> 53.8 us (0.30)
  the two profiles are of different devices: /device:TPU:0 before, /device:TPU:3 now
where the time goes in v2:
time: 53.8 us; the launch traced here: 53.6 us
  Pallas kernels  52.1 us (97%)
  local copies, waits for them, and re-layouts  1.57 us (3%)
    pallas_call x1, Pallas kernels, shards(): pl.pallas_call(functools.partial(kernel, n), out_shape=jax.ShapeDtypeStru...  52.1 us
    unnamed x1, local copies, waits for them, and re-layouts  1.57 us

profile of v2, /device:TPU:3, one launch (start us, length us, event | category | flops | bytes accessed | tf_op | source)
XLA Modules:
  0.0 53.6 jit_solution(10955177111391453699)
XLA Ops:
  0.0 52.1 %shard_map.37 = bf16[1,64,1024]{2,1,0:T(8,128)(2,1)} custom-call(s32[1,128]{1,0:T(1,128)} %bitcast.1, bf16[1,1024,1024]{2,1,0:T(8,128)(2,1)} %trans_ref.1, bf16[1,1024,1024]{2,1,0:T(8,128)(2,1)} %refl_ref.1), custom_call_target="tpu_custom_call" | custom-call | tf_op jit(solution)/shard_map/pallas_call | solution.py:336
  52.1 1.6 %copy.5 = bf16[1,64,1024]{2,1,0:T(8,128)(2,1)} copy(bf16[1,64,1024]{2,1,0:T(8,128)(2,1)} %shard_map.37) | data formatting | bytes 262144

commit v3 on v2

--- a/solution.py
+++ b/solution.py
@@ -28,9 +28,9 @@
 
 def kernel(
     n, modes_ref, trans_ref, refl_ref, out_ref,
-    upper_t, lower_t, upper_r, lower_r, merged, merged_t, inner,
-    down_in, down_out, up_in, up_out, half_in, echo,
-    local_sem, tile_send, tile_recv, pair_send, pair_recv, echo_sem,
+    upper_t, lower_t, upper_r, lower_r, merged, merged_t, inner, odd_t, pair_t,
+    down_in, down_out, up_in, up_out, odd_out, odd_echo, half_in, echo,
+    local_sem, odd_send, odd_recv, odd_echo_sem, side_send, tile_send, tile_recv, pair_send, pair_recv, echo_sem,
     down_send, down_recv, pass_send, up_send, up_recv, half_send, half_recv,
 ):
     me = lax.axis_index("sec")
@@ -44,11 +44,12 @@
     not_last = jnp.logical_not(is_last)
     on_zero = parity == 0
     on_one = parity == 1
-    is_chain = jnp.logical_and(on_one, not_last)
-    is_echo = jnp.logical_and(on_zero, not_last)
-    is_turn = jnp.logical_and(on_zero, is_last)
+    even = section % 2 == 0
+    odd = section % 2 == 1
+    paired = section < sections - 2
     below = lax.rem(jnp.where(section == sections - 2, me + 1, me + 2), n)
-    above = lax.rem(me + n - 1 - parity, n)
+    above = lax.rem(me + n - 1 - 3 * parity, n)
+    beside = lax.rem(me + n - 2, n)
     modes = upper_t.shape[0]
     tiles = modes // TILE
     batches = down_in.shape[0] // ROWS
@@ -85,19 +86,43 @@
     def greet(device):
         pl.semaphore_signal(barrier, inc=1, device_id={"sec": device}, device_id_type=MESH)
 
-    has_below = is_chain
-    has_above = jnp.logical_or(is_turn, jnp.logical_and(is_chain, not_first))
     greet(partner)
-
-    @pl.when(has_above)
+    zero_odd = jnp.logical_and(on_zero, odd)
+    one_even = jnp.logical_and(on_one, even)
+    one_odd = jnp.logical_and(jnp.logical_and(on_one, odd), not_last)
+    even_paired = jnp.logical_and(one_even, paired)
+    even_inside = jnp.logical_and(one_even, not_first)
+
+    @pl.when(zero_odd)
     def _():
         greet(above)
 
-    @pl.when(has_below)
-    def _():
-        greet(below)
-
-    peers = 1 + has_above.astype(jnp.int32) + has_below.astype(jnp.int32)
+    @pl.when(one_even)
+    def _():
+        greet(me + 1)
+
+    @pl.when(even_paired)
+    def _():
+        greet(lax.rem(me + 2, n))
+        greet(lax.rem(me + 4, n))
+
+    @pl.when(even_inside)
+    def _():
+        greet(beside)
+        greet(above)
+
+    @pl.when(one_odd)
+    def _():
+        greet(beside)
+        greet(lax.rem(me + 2, n))
+
+    def number(flag):
+        return flag.astype(jnp.int32)
+
+    peers = (
+        1 + number(zero_odd) + number(one_even)
+        + 2 * (number(even_paired) + number(even_inside) + number(one_odd))
+    )
     pl.semaphore_wait(barrier, peers)
 
     def tile_copy(tile):
@@ -132,6 +157,20 @@
             up_out.at[batch_rows(batch), :], up_in.at[batch_rows(batch), :],
             up_send.at[batch], up_recv.at[batch], above,
         )
+
+    def side_copy(batch):
+        return remote(
+            up_out.at[batch_rows(batch), :], up_in.at[batch_rows(batch), :],
+            side_send.at[batch], up_recv.at[batch], beside,
+        )
+
+    def odd_copy(tile):
+        return remote(
+            merged_t.at[tile_rows(tile), :], odd_t.at[tile_rows(tile), :],
+            odd_send.at[tile], odd_recv.at[tile], beside,
+        )
+
+    odd_echo_copy = remote(odd_out, odd_echo, odd_echo_sem.at[0], odd_echo_sem.at[1], above)
 
     def half_copy(place):
         batch = (1 - parity) * half_batches + place
@@ -219,8 +258,14 @@
             field = down_in[...]
             middle = nn(field, upper_t[...]).astype(BF16)
             lower = nn(middle, lower_r[...]).astype(BF16)
-            echo[...] = nn(field, upper_r[...]) + nn(lower, merged_t[...])
+            value = nn(field, upper_r[...]) + nn(lower, merged_t[...])
+            echo[...] = value
+            odd_out[...] = value.astype(BF16)
             give_echo.start()
+
+            @pl.when(odd)
+            def _():
+                odd_echo_copy.start()
 
             @pl.when(is_first)
             def _():
@@ -229,6 +274,10 @@
             each(half_batches, lambda place: half_copy(place).wait_recv())
             out_ref[0] = half_in[...]
             give_echo.wait_send()
+
+            @pl.when(odd)
+            def _():
+                odd_echo_copy.wait_send()
 
         each(tiles, lambda tile: tile_copy(tile).wait_send())
 
@@ -276,6 +325,10 @@
 
         each(tiles, merge_tile)
 
+        @pl.when(one_odd)
+        def _():
+            each(tiles, lambda tile: odd_copy(tile).start())
+
         @pl.when(jnp.logical_and(section > 1, not_last))
         def _():
             def go(batch):
@@ -291,28 +344,59 @@
         def _():
             give_echo.wait_recv()
 
-            def go(batch):
-                rows = batch_rows(batch)
-                up_copy(batch).wait_recv()
-                up_out[rows, :] = (echo[rows, :] + nn(up_in[rows, :], merged_t[...])).astype(BF16)
-
-                @pl.when(not_first)
-                def _():
-                    up_copy(batch).start()
-
-                @pl.when(batch < half_batches)
-                def _():
-                    half_copy(batch).start()
-
-            each(batches, go)
+            @pl.when(even_paired)
+            def _():
+                odd_echo_copy.wait_recv()
+                echo[...] += nn(odd_echo[...], merged_t[...])
+
+                def pair_tile(tile):
+                    rows = tile_rows(tile)
+                    odd_copy(tile).wait_recv()
+                    pair_t[rows, :] = nn(odd_t[rows, :], merged_t[...]).astype(BF16)
+
+                each(tiles, pair_tile)
+
+            def climb(step_t):
+                def go(batch):
+                    rows = batch_rows(batch)
+                    up_copy(batch).wait_recv()
+                    up_out[rows, :] = (echo[rows, :] + nn(up_in[rows, :], step_t[...])).astype(BF16)
+
+                    @pl.when(even_inside)
+                    def _():
+                        up_copy(batch).start()
+                        side_copy(batch).start()
+
+                    @pl.when(batch < half_batches)
+                    def _():
+                        half_copy(batch).start()
+
+                each(batches, go)
+
+            @pl.when(even_paired)
+            def _():
+                climb(pair_t)
+
+            @pl.when(jnp.logical_not(even_paired))
+            def _():
+                climb(merged_t)
+
             own_half()
             each(batches, lambda batch: down_copy(batch).wait_send())
             each(half_batches, lambda place: half_copy(place).wait_send())
 
             @pl.when(not_first)
             def _():
+                each(batches, lambda batch: pass_copy(batch).wait_send())
+
+            @pl.when(even_inside)
+            def _():
                 each(batches, lambda batch: up_copy(batch).wait_send())
-                each(batches, lambda batch: pass_copy(batch).wait_send())
+                each(batches, lambda batch: side_copy(batch).wait_send())
+
+            @pl.when(one_odd)
+            def _():
+                each(tiles, lambda tile: odd_copy(tile).wait_send())
 
         @pl.when(is_last)
         def _():
@@ -338,7 +422,9 @@
         out_shape=jax.ShapeDtypeStruct((1, half, modes), BF16),
         in_specs=[vmem, anywhere, anywhere],
         out_specs=vmem,
-        scratch_shapes=[pltpu.VMEM(square, BF16)] * 7 + [
+        scratch_shapes=[pltpu.VMEM(square, BF16)] * 9 + [
+            pltpu.VMEM((count, modes), BF16),
+            pltpu.VMEM((count, modes), BF16),
             pltpu.VMEM((count, modes), BF16),
             pltpu.VMEM((count, modes), BF16),
             pltpu.VMEM((count, modes), BF16),
@@ -346,6 +432,10 @@
             pltpu.VMEM((half, modes), BF16),
             pltpu.VMEM((count, modes), F32),
             pltpu.SemaphoreType.DMA((2,)),
+            tiles,
+            tiles,
+            pltpu.SemaphoreType.DMA((2,)),
+            per_batch,
             tiles,
             tiles,
             pltpu.SemaphoreType.DMA,

time: 53.8 us -> 52.3 us (0.972)
  the two profiles are of different devices: /device:TPU:3 before, /device:TPU:7 now
where the time goes in v3:
time: 52.3 us; the launch traced here: 52 us
  Pallas kernels  50.5 us (97%)
  local copies, waits for them, and re-layouts  1.57 us (3%)
    pallas_call x1, Pallas kernels, shards(): pl.pallas_call(functools.partial(kernel, n), out_shape=jax.ShapeDtypeStru...  50.5 us
    unnamed x1, local copies, waits for them, and re-layouts  1.57 us

profile of v3, /device:TPU:7, one launch (start us, length us, event | category | flops | bytes accessed | tf_op | source)
XLA Modules:
  0.0 52.0 jit_solution(3008827941542287532)
XLA Ops:
  0.0 50.5 %shard_map.37 = bf16[1,64,1024]{2,1,0:T(8,128)(2,1)} custom-call(s32[1,128]{1,0:T(1,128)} %bitcast.1, bf16[1,1024,1024]{2,1,0:T(8,128)(2,1)} %trans_ref.1, bf16[1,1024,1024]{2,1,0:T(8,128)(2,1)} %refl_ref.1), custom_call_target="tpu_custom_call" | custom-call | tf_op jit(solution)/shard_map/pallas_call | solution.py:420
  50.5 1.6 %copy.5 = bf16[1,64,1024]{2,1,0:T(8,128)(2,1)} copy(bf16[1,64,1024]{2,1,0:T(8,128)(2,1)} %shard_map.37) | data formatting | bytes 262144

commit v4 on v3

--- a/solution.py
+++ b/solution.py
@@ -27,10 +27,10 @@
 
 
 def kernel(
-    n, modes_ref, trans_ref, refl_ref, out_ref,
+    n, groups, modes_ref, trans_ref, refl_ref, out_ref,
     upper_t, lower_t, upper_r, lower_r, merged, merged_t, inner, odd_t, pair_t,
     down_in, down_out, up_in, up_out, odd_out, odd_echo, half_in, echo,
-    local_sem, odd_send, odd_recv, odd_echo_sem, side_send, tile_send, tile_recv, pair_send, pair_recv, echo_sem,
+    local_sem, odd_send, odd_recv, odd_echo_sem, mate_send, mate_recv, side_send, tile_send, tile_recv, pair_send, pair_recv, echo_sem,
     down_send, down_recv, pass_send, up_send, up_recv, half_send, half_recv,
 ):
     me = lax.axis_index("sec")
@@ -44,6 +44,9 @@
     not_last = jnp.logical_not(is_last)
     on_zero = parity == 0
     on_one = parity == 1
+    shared = groups % 2 == 0
+    group = lax.axis_index("freq")
+    mate = group + 1 - 2 * (group % 2) if shared else group
     even = section % 2 == 0
     odd = section % 2 == 1
     paired = section < sections - 2
@@ -52,6 +55,9 @@
     beside = lax.rem(me + n - 2, n)
     modes = upper_t.shape[0]
     tiles = modes // TILE
+    own_tiles = tiles // 2 if shared else tiles
+    first_own = (group % 2) * own_tiles if shared else 0
+    first_other = own_tiles - first_own
     batches = down_in.shape[0] // ROWS
     half_batches = batches // 2
     half = half_in.shape[0]
@@ -105,6 +111,10 @@
     def _():
         greet(lax.rem(me + 2, n))
         greet(lax.rem(me + 4, n))
+        if shared:
+            pl.semaphore_signal(
+                barrier, inc=1, device_id={"freq": mate, "sec": me}, device_id_type=MESH
+            )
 
     @pl.when(even_inside)
     def _():
@@ -121,7 +131,7 @@
 
     peers = (
         1 + number(zero_odd) + number(one_even)
-        + 2 * (number(even_paired) + number(even_inside) + number(one_odd))
+        + 2 * (number(even_inside) + number(one_odd)) + (3 if shared else 2) * number(even_paired)
     )
     pl.semaphore_wait(barrier, peers)
 
@@ -168,6 +178,13 @@
         return remote(
             merged_t.at[tile_rows(tile), :], odd_t.at[tile_rows(tile), :],
             odd_send.at[tile], odd_recv.at[tile], beside,
+        )
+
+    def mate_copy(tile):
+        return pltpu.make_async_remote_copy(
+            src_ref=pair_t.at[tile_rows(tile), :], dst_ref=pair_t.at[tile_rows(tile), :],
+            send_sem=mate_send.at[tile], recv_sem=mate_recv.at[tile],
+            device_id={"freq": mate, "sec": me}, device_id_type=MESH,
         )
 
     odd_echo_copy = remote(odd_out, odd_echo, odd_echo_sem.at[0], odd_echo_sem.at[1], above)
@@ -327,7 +344,21 @@
 
         @pl.when(one_odd)
         def _():
-            each(tiles, lambda tile: odd_copy(tile).start())
+            each(own_tiles, lambda place: odd_copy(first_own + place).start())
+
+        def pair_tile(place):
+            tile = first_own + place
+            rows = tile_rows(tile)
+            odd_copy(tile).wait_recv()
+            pair_t[rows, :] = nn(odd_t[rows, :], merged_t[...]).astype(BF16)
+            if shared:
+                mate_copy(tile).start()
+
+        early = section >= 4
+
+        @pl.when(jnp.logical_and(even_paired, early))
+        def _():
+            pair_tile(0)
 
         @pl.when(jnp.logical_and(section > 1, not_last))
         def _():
@@ -342,19 +373,22 @@
 
         @pl.when(not_last)
         def _():
-            give_echo.wait_recv()
+            @pl.when(jnp.logical_not(even_paired))
+            def _():
+                give_echo.wait_recv()
 
             @pl.when(even_paired)
             def _():
+                @pl.when(jnp.logical_not(early))
+                def _():
+                    pair_tile(0)
+
+                each(own_tiles - 1, lambda place: pair_tile(place + 1))
+                give_echo.wait_recv()
                 odd_echo_copy.wait_recv()
                 echo[...] += nn(odd_echo[...], merged_t[...])
-
-                def pair_tile(tile):
-                    rows = tile_rows(tile)
-                    odd_copy(tile).wait_recv()
-                    pair_t[rows, :] = nn(odd_t[rows, :], merged_t[...]).astype(BF16)
-
-                each(tiles, pair_tile)
+                if shared:
+                    each(own_tiles, lambda place: mate_copy(first_other + place).wait_recv())
 
             def climb(step_t):
                 def go(batch):
@@ -396,7 +430,12 @@
 
             @pl.when(one_odd)
             def _():
-                each(tiles, lambda tile: odd_copy(tile).wait_send())
+                each(own_tiles, lambda place: odd_copy(first_own + place).wait_send())
+
+            if shared:
+                @pl.when(even_paired)
+                def _():
+                    each(own_tiles, lambda place: mate_copy(first_own + place).wait_send())
 
         @pl.when(is_last)
         def _():
@@ -406,7 +445,7 @@
         share_r.wait_send()
 
 
-def shards(n, layer_trans, layer_refl, source_modes):
+def shards(n, groups, layer_trans, layer_refl, source_modes):
     modes = layer_trans.shape[1]
     count = source_modes.shape[0]
     half = count // 2
@@ -418,7 +457,7 @@
     per_batch = pltpu.SemaphoreType.DMA((batches,))
     per_half = pltpu.SemaphoreType.DMA((batches // 2,))
     return pl.pallas_call(
-        functools.partial(kernel, n),
+        functools.partial(kernel, n, groups),
         out_shape=jax.ShapeDtypeStruct((1, half, modes), BF16),
         in_specs=[vmem, anywhere, anywhere],
         out_specs=vmem,
@@ -435,6 +474,8 @@
             tiles,
             tiles,
             pltpu.SemaphoreType.DMA((2,)),
+            tiles,
+            tiles,
             per_batch,
             tiles,
             tiles,
@@ -457,7 +498,7 @@
 
 def solution(mesh):
     return jax.shard_map(
-        functools.partial(shards, mesh.shape["sec"]),
+        functools.partial(shards, mesh.shape["sec"], mesh.shape["freq"]),
         mesh=mesh,
         in_specs=(P("sec", None, None), P("sec", None, None), P("freq")),
         out_specs=P(("freq", "sec"), None, None),

time: 52.3 us -> 47 us (0.90)
  Pallas kernels: 50.5 us -> 45.3 us
    pallas_call x1, Pallas kernels: 50.5 us -> 45.3 us  [shards(): pl.pallas_call(functools.partial(kernel, n, groups), out_shape=jax.ShapeD...]
where the time goes in v4:
time: 47 us; the launch traced here: 46.8 us
  Pallas kernels  45.3 us (96%)
  local copies, waits for them, and re-layouts  1.57 us (3%)
    pallas_call x1, Pallas kernels, shards(): pl.pallas_call(functools.partial(kernel, n, groups), out_shape=jax.ShapeD...  45.3 us
    unnamed x1, local copies, waits for them, and re-layouts  1.57 us

profile of v4, /device:TPU:7, one launch (start us, length us, event | category | flops | bytes accessed | tf_op | source)
XLA Modules:
  0.0 46.8 jit_solution(1894520822782558562)
XLA Ops:
  0.0 45.3 %shard_map.37 = bf16[1,64,1024]{2,1,0:T(8,128)(2,1)} custom-call(s32[1,128]{1,0:T(1,128)} %bitcast.1, bf16[1,1024,1024]{2,1,0:T(8,128)(2,1)} %trans_ref.1, bf16[1,1024,1024]{2,1,0:T(8,128)(2,1)} %refl_ref.1), custom_call_target="tpu_custom_call" | custom-call | tf_op jit(solution)/shard_map/pallas_call | solution.py:459
  45.3 1.6 %copy.5 = bf16[1,64,1024]{2,1,0:T(8,128)(2,1)} copy(bf16[1,64,1024]{2,1,0:T(8,128)(2,1)} %shard_map.37) | data formatting | bytes 262144

commit v5 on v4

--- a/solution.py
+++ b/solution.py
@@ -9,6 +9,7 @@
 
 ROWS = 32
 TILE = 256
+PIECE = 128
 F32 = jnp.float32
 BF16 = jnp.bfloat16
 MESH = pl.DeviceIdType.MESH
@@ -28,9 +29,9 @@
 
 def kernel(
     n, groups, modes_ref, trans_ref, refl_ref, out_ref,
-    upper_t, lower_t, upper_r, lower_r, merged, merged_t, inner, odd_t, pair_t,
+    upper_t, lower_t, upper_r, lower_r, merged, merged_t, odd_t, pair_t,
     down_in, down_out, up_in, up_out, odd_out, odd_echo, half_in, echo,
-    local_sem, odd_send, odd_recv, odd_echo_sem, mate_send, mate_recv, side_send, tile_send, tile_recv, pair_send, pair_recv, echo_sem,
+    local_sem, odd_send, odd_recv, odd_echo_send, odd_echo_recv, piece_send, piece_recv, swap_send, swap_recv, mate_send, mate_recv, side_send, tile_send, tile_recv, pair_send, pair_recv, echo_send, echo_recv,
     down_send, down_recv, pass_send, up_send, up_recv, half_send, half_recv,
 ):
     me = lax.axis_index("sec")
@@ -50,6 +51,7 @@
     even = section % 2 == 0
     odd = section % 2 == 1
     paired = section < sections - 2
+    is_turn = section == sections - 2
     below = lax.rem(jnp.where(section == sections - 2, me + 1, me + 2), n)
     above = lax.rem(me + n - 1 - 3 * parity, n)
     beside = lax.rem(me + n - 2, n)
@@ -106,16 +108,16 @@
     @pl.when(one_even)
     def _():
         greet(me + 1)
-
-    @pl.when(even_paired)
-    def _():
-        greet(lax.rem(me + 2, n))
-        greet(lax.rem(me + 4, n))
         if shared:
             pl.semaphore_signal(
                 barrier, inc=1, device_id={"freq": mate, "sec": me}, device_id_type=MESH
             )
 
+    @pl.when(even_paired)
+    def _():
+        greet(lax.rem(me + 2, n))
+        greet(lax.rem(me + 4, n))
+
     @pl.when(even_inside)
     def _():
         greet(beside)
@@ -130,8 +132,8 @@
         return flag.astype(jnp.int32)
 
     peers = (
-        1 + number(zero_odd) + number(one_even)
-        + 2 * (number(even_inside) + number(one_odd)) + (3 if shared else 2) * number(even_paired)
+        1 + number(zero_odd) + (2 if shared else 1) * number(one_even)
+        + 2 * (number(even_paired) + number(even_inside) + number(one_odd))
     )
     pl.semaphore_wait(barrier, peers)
 
@@ -142,7 +144,6 @@
         )
 
     share_r = remote(refl_ref.at[0], lower_r, pair_send, pair_recv, partner)
-    give_echo = remote(echo, echo, echo_sem.at[0], echo_sem.at[1], partner)
 
     def down_copy(batch):
         return remote(
@@ -187,7 +188,39 @@
             device_id={"freq": mate, "sec": me}, device_id_type=MESH,
         )
 
-    odd_echo_copy = remote(odd_out, odd_echo, odd_echo_sem.at[0], odd_echo_sem.at[1], above)
+    own_pieces = modes // PIECE // 2 if shared else modes // PIECE
+    first_piece = (group % 2) * own_pieces if shared else 0
+    other_piece = own_pieces - first_piece
+
+    def piece_rows(piece):
+        return pl.ds(pl.multiple_of(piece * PIECE, PIECE), PIECE)
+
+    def piece_copy(piece):
+        rows = piece_rows(piece)
+        return remote(
+            merged.at[rows, :], odd_t.at[rows, :], piece_send.at[piece], piece_recv.at[piece], above,
+        )
+
+    def swap_copy(piece):
+        rows = piece_rows(piece)
+        return pltpu.make_async_remote_copy(
+            src_ref=odd_t.at[rows, :], dst_ref=odd_t.at[rows, :],
+            send_sem=swap_send.at[piece], recv_sem=swap_recv.at[piece],
+            device_id={"freq": mate, "sec": me}, device_id_type=MESH,
+        )
+
+    def echo_copy(batch):
+        rows = batch_rows(batch)
+        return remote(
+            echo.at[rows, :], echo.at[rows, :], echo_send.at[batch], echo_recv.at[batch], partner,
+        )
+
+    def odd_echo_copy(batch):
+        rows = batch_rows(batch)
+        return remote(
+            odd_out.at[rows, :], odd_echo.at[rows, :],
+            odd_echo_send.at[batch], odd_echo_recv.at[batch], above,
+        )
 
     def half_copy(place):
         batch = (1 - parity) * half_batches + place
@@ -238,63 +271,70 @@
         load_r0.wait()
         share_r.wait_recv()
 
+        def refl_tile(tile):
+            rows = tile_rows(tile)
+            half_way = nn(upper_t[rows, :], lower_r[...]).astype(BF16)
+            merged[rows, :] = (
+                upper_r[rows, :].astype(F32) + nn(half_way, merged_t[...])
+            ).astype(BF16)
+
+        def own_tile(place):
+            tile = first_own + place
+            refl_tile(tile)
+
+            @pl.when(is_last)
+            def _():
+                each(TILE // PIECE, lambda part: piece_copy(tile * (TILE // PIECE) + part).start())
+
+        each(own_tiles, own_tile)
+        if shared:
+            each(own_tiles, lambda place: refl_tile(first_other + place))
+
+        def reflect(batch):
+            rows = batch_rows(batch)
+
+            @pl.when(not_first)
+            def _():
+                pass_copy(batch).wait_recv()
+
+            value = nn(down_in[rows, :], merged[...])
+            up_out[rows, :] = value.astype(BF16)
+
+            @pl.when(not_last)
+            def _():
+                echo[rows, :] = value
+                odd_out[rows, :] = value.astype(BF16)
+                echo_copy(batch).start()
+
+                @pl.when(odd)
+                def _():
+                    odd_echo_copy(batch).start()
+
+            @pl.when(jnp.logical_and(is_last, batch >= half_batches))
+            def _():
+                half_copy(batch - half_batches).start()
+
+        each(batches, reflect)
+
         @pl.when(is_last)
         def _():
-            def inner_tile(tile):
-                rows = tile_rows(tile)
-                inner[rows, :] = nn(lower_r[rows, :], merged_t[...]).astype(BF16)
-
-            each(tiles, inner_tile)
-
-            def refl_tile(tile):
-                rows = tile_rows(tile)
-                merged[rows, :] = (
-                    upper_r[rows, :].astype(F32) + nn(upper_t[rows, :], inner[...])
-                ).astype(BF16)
-
-            each(tiles, refl_tile)
-
-            def go(batch):
-                rows = batch_rows(batch)
-                down_copy(batch).wait_recv()
-                up_out[rows, :] = nn(down_in[rows, :], merged[...]).astype(BF16)
-                up_copy(batch).start()
-
-            each(batches, go)
-            each(half_batches, lambda place: half_copy(place).start())
             own_half()
-            each(batches, lambda batch: up_copy(batch).wait_send())
             each(half_batches, lambda place: half_copy(place).wait_send())
+            each(own_pieces, lambda place: piece_copy(first_piece + place).wait_send())
 
         @pl.when(not_last)
         def _():
-            @pl.when(not_first)
-            def _():
-                each(batches, lambda batch: pass_copy(batch).wait_recv())
-
-            field = down_in[...]
-            middle = nn(field, upper_t[...]).astype(BF16)
-            lower = nn(middle, lower_r[...]).astype(BF16)
-            value = nn(field, upper_r[...]) + nn(lower, merged_t[...])
-            echo[...] = value
-            odd_out[...] = value.astype(BF16)
-            give_echo.start()
-
-            @pl.when(odd)
-            def _():
-                odd_echo_copy.start()
-
             @pl.when(is_first)
             def _():
                 each(batches, lambda batch: middle_copy(batch).wait_send())
 
             each(half_batches, lambda place: half_copy(place).wait_recv())
             out_ref[0] = half_in[...]
-            give_echo.wait_send()
+            each(batches, lambda batch: echo_copy(batch).wait_send())
 
             @pl.when(odd)
             def _():
-                odd_echo_copy.wait_send()
+                each(batches, lambda batch: odd_echo_copy(batch).wait_send())
 
         each(tiles, lambda tile: tile_copy(tile).wait_send())
 
@@ -360,23 +400,41 @@
         def _():
             pair_tile(0)
 
+        @pl.when(jnp.logical_and(on_one, is_turn))
+        def _():
+            def swap(place):
+                piece = first_piece + place
+                piece_copy(piece).wait_recv()
+                if shared:
+                    swap_copy(piece).start()
+
+            each(own_pieces, swap)
+
         @pl.when(jnp.logical_and(section > 1, not_last))
         def _():
             def go(batch):
                 rows = batch_rows(batch)
                 down_copy(batch).wait_recv()
+
+                @pl.when(is_turn)
+                def _():
+                    pass_copy(batch).start()
+
                 down_out[rows, :] = nn(down_in[rows, :], merged[...]).astype(BF16)
                 down_copy(batch).start()
-                pass_copy(batch).start()
+
+                @pl.when(paired)
+                def _():
+                    pass_copy(batch).start()
+
+                @pl.when(jnp.logical_and(odd, jnp.logical_not(paired)))
+                def _():
+                    pass_copy(batch).start()
 
             each(batches, go)
 
         @pl.when(not_last)
         def _():
-            @pl.when(jnp.logical_not(even_paired))
-            def _():
-                give_echo.wait_recv()
-
             @pl.when(even_paired)
             def _():
                 @pl.when(jnp.logical_not(early))
@@ -384,16 +442,30 @@
                     pair_tile(0)
 
                 each(own_tiles - 1, lambda place: pair_tile(place + 1))
-                give_echo.wait_recv()
-                odd_echo_copy.wait_recv()
+                each(batches, lambda batch: echo_copy(batch).wait_recv())
+                each(batches, lambda batch: odd_echo_copy(batch).wait_recv())
                 echo[...] += nn(odd_echo[...], merged_t[...])
                 if shared:
                     each(own_tiles, lambda place: mate_copy(first_other + place).wait_recv())
 
+            @pl.when(is_turn)
+            def _():
+                if shared:
+                    each(own_pieces, lambda place: swap_copy(other_piece + place).wait_recv())
+                up_in[...] = nn(down_out[...], odd_t[...]).astype(BF16)
+
             def climb(step_t):
                 def go(batch):
                     rows = batch_rows(batch)
-                    up_copy(batch).wait_recv()
+
+                    @pl.when(jnp.logical_not(even_paired))
+                    def _():
+                        echo_copy(batch).wait_recv()
+
+                    @pl.when(jnp.logical_not(is_turn))
+                    def _():
+                        up_copy(batch).wait_recv()
+
                     up_out[rows, :] = (echo[rows, :] + nn(up_in[rows, :], step_t[...])).astype(BF16)
 
                     @pl.when(even_inside)
@@ -436,6 +508,10 @@
                 @pl.when(even_paired)
                 def _():
                     each(own_tiles, lambda place: mate_copy(first_own + place).wait_send())
+
+                @pl.when(is_turn)
+                def _():
+                    each(own_pieces, lambda place: swap_copy(first_piece + place).wait_send())
 
         @pl.when(is_last)
         def _():
@@ -454,6 +530,7 @@
     vmem = pl.BlockSpec(memory_space=pltpu.VMEM)
     anywhere = pl.BlockSpec(memory_space=pl.ANY)
     tiles = pltpu.SemaphoreType.DMA((modes // TILE,))
+    pieces = pltpu.SemaphoreType.DMA((modes // PIECE,))
     per_batch = pltpu.SemaphoreType.DMA((batches,))
     per_half = pltpu.SemaphoreType.DMA((batches // 2,))
     return pl.pallas_call(
@@ -461,7 +538,7 @@
         out_shape=jax.ShapeDtypeStruct((1, half, modes), BF16),
         in_specs=[vmem, anywhere, anywhere],
         out_specs=vmem,
-        scratch_shapes=[pltpu.VMEM(square, BF16)] * 9 + [
+        scratch_shapes=[pltpu.VMEM(square, BF16)] * 8 + [
             pltpu.VMEM((count, modes), BF16),
             pltpu.VMEM((count, modes), BF16),
             pltpu.VMEM((count, modes), BF16),
@@ -473,7 +550,12 @@
             pltpu.SemaphoreType.DMA((2,)),
             tiles,
             tiles,
-            pltpu.SemaphoreType.DMA((2,)),
+            per_batch,
+            per_batch,
+            pieces,
+            pieces,
+            pieces,
+            pieces,
             tiles,
             tiles,
             per_batch,
@@ -481,7 +563,8 @@
             tiles,
             pltpu.SemaphoreType.DMA,
             pltpu.SemaphoreType.DMA,
-            pltpu.SemaphoreType.DMA((2,)),
+            per_batch,
+            per_batch,
             per_batch,
             per_batch,
             per_batch,

time: 47 us -> 46.8 us (level)
  no operation moved by 1% of the time
where the time goes in v5:
time: 46.8 us; the launch traced here: 46.7 us
  Pallas kernels  45.1 us (96%)
  local copies, waits for them, and re-layouts  1.57 us (3%)
    pallas_call x1, Pallas kernels, shards(): pl.pallas_call(functools.partial(kernel, n, groups), out_shape=jax.ShapeD...  45.1 us
    unnamed x1, local copies, waits for them, and re-layouts  1.57 us

profile of v5, /device:TPU:7, one launch (start us, length us, event | category | flops | bytes accessed | tf_op | source)
XLA Modules:
  0.0 46.7 jit_solution(11232451546766912204)
XLA Ops:
  0.0 45.1 %shard_map.37 = bf16[1,64,1024]{2,1,0:T(8,128)(2,1)} custom-call(s32[1,128]{1,0:T(1,128)} %bitcast.1, bf16[1,1024,1024]{2,1,0:T(8,128)(2,1)} %trans_ref.1, bf16[1,1024,1024]{2,1,0:T(8,128)(2,1)} %refl_ref.1), custom_call_target="tpu_custom_call" | custom-call | tf_op jit(solution)/shard_map/pallas_call | solution.py:536
  45.1 1.6 %copy.5 = bf16[1,64,1024]{2,1,0:T(8,128)(2,1)} copy(bf16[1,64,1024]{2,1,0:T(8,128)(2,1)} %shard_map.37) | data formatting | bytes 262144

commit v6 on v5

--- a/solution.py
+++ b/solution.py
@@ -31,7 +31,7 @@
     n, groups, modes_ref, trans_ref, refl_ref, out_ref,
     upper_t, lower_t, upper_r, lower_r, merged, merged_t, odd_t, pair_t,
     down_in, down_out, up_in, up_out, odd_out, odd_echo, half_in, echo,
-    local_sem, odd_send, odd_recv, odd_echo_send, odd_echo_recv, piece_send, piece_recv, swap_send, swap_recv, mate_send, mate_recv, side_send, tile_send, tile_recv, pair_send, pair_recv, echo_send, echo_recv,
+    local_sem, odd_send, odd_recv, odd_echo_send, odd_echo_recv, piece_send, piece_recv, swap_send, swap_recv, mate_send, mate_recv, forward_send, side_send, tile_send, tile_recv, pair_send, pair_recv, echo_send, echo_recv,
     down_send, down_recv, pass_send, up_send, up_recv, half_send, half_recv,
 ):
     me = lax.axis_index("sec")
@@ -175,6 +175,12 @@
             side_send.at[batch], up_recv.at[batch], beside,
         )
 
+    def forward_copy(batch):
+        return remote(
+            up_in.at[batch_rows(batch), :], up_in.at[batch_rows(batch), :],
+            forward_send.at[batch], up_recv.at[batch], lax.rem(me + 2, n),
+        )
+
     def odd_copy(tile):
         return remote(
             merged_t.at[tile_rows(tile), :], odd_t.at[tile_rows(tile), :],
@@ -466,12 +472,15 @@
                     def _():
                         up_copy(batch).wait_recv()
 
+                    @pl.when(jnp.logical_and(even_paired, batch < half_batches))
+                    def _():
+                        forward_copy(batch).start()
+
                     up_out[rows, :] = (echo[rows, :] + nn(up_in[rows, :], step_t[...])).astype(BF16)
 
                     @pl.when(even_inside)
                     def _():
                         up_copy(batch).start()
-                        side_copy(batch).start()
 
                     @pl.when(batch < half_batches)
                     def _():
@@ -479,6 +488,10 @@
 
                 each(batches, go)
 
+                @pl.when(even_inside)
+                def _():
+                    each(half_batches, lambda place: side_copy(half_batches + place).start())
+
             @pl.when(even_paired)
             def _():
                 climb(pair_t)
@@ -498,7 +511,11 @@
             @pl.when(even_inside)
             def _():
                 each(batches, lambda batch: up_copy(batch).wait_send())
-                each(batches, lambda batch: side_copy(batch).wait_send())
+                each(half_batches, lambda place: side_copy(half_batches + place).wait_send())
+
+            @pl.when(even_paired)
+            def _():
+                each(half_batches, lambda batch: forward_copy(batch).wait_send())
 
             @pl.when(one_odd)
             def _():
@@ -558,6 +575,7 @@
             pieces,
             tiles,
             tiles,
+            per_half,
             per_batch,
             tiles,
             tiles,

time: 46.8 us -> 46.9 us (level)
  no operation moved by 1% of the time
where the time goes in v6:
time: 46.9 us; the launch traced here: 46.8 us
  Pallas kernels  45.2 us (96%)
  local copies, waits for them, and re-layouts  1.57 us (3%)
    pallas_call x1, Pallas kernels, shards(): pl.pallas_call(functools.partial(kernel, n, groups), out_shape=jax.ShapeD...  45.2 us
    unnamed x1, local copies, waits for them, and re-layouts  1.57 us

profile of v6, /device:TPU:7, one launch (start us, length us, event | category | flops | bytes accessed | tf_op | source)
XLA Modules:
  0.0 46.8 jit_solution(15535518151084719485)
XLA Ops:
  0.0 45.2 %shard_map.37 = bf16[1,64,1024]{2,1,0:T(8,128)(2,1)} custom-call(s32[1,128]{1,0:T(1,128)} %bitcast.1, bf16[1,1024,1024]{2,1,0:T(8,128)(2,1)} %trans_ref.1, bf16[1,1024,1024]{2,1,0:T(8,128)(2,1)} %refl_ref.1), custom_call_target="tpu_custom_call" | custom-call | tf_op jit(solution)/shard_map/pallas_call | solution.py:553
  45.2 1.6 %copy.5 = bf16[1,64,1024]{2,1,0:T(8,128)(2,1)} copy(bf16[1,64,1024]{2,1,0:T(8,128)(2,1)} %shard_map.37) | data formatting | bytes 262144

commit v7 on v6

--- a/solution.py
+++ b/solution.py
@@ -67,6 +67,13 @@
     def tile_rows(tile):
         return pl.ds(pl.multiple_of(tile * TILE, TILE), TILE)
 
+    own_pieces = modes // PIECE // 2 if shared else modes // PIECE
+    first_piece = (group % 2) * own_pieces if shared else 0
+    other_piece = own_pieces - first_piece
+
+    def piece_rows(piece):
+        return pl.ds(pl.multiple_of(piece * PIECE, PIECE), PIECE)
+
     def batch_rows(batch):
         return pl.ds(pl.multiple_of(batch * ROWS, ROWS), ROWS)
 
@@ -181,25 +188,19 @@
             forward_send.at[batch], up_recv.at[batch], lax.rem(me + 2, n),
         )
 
-    def odd_copy(tile):
-        return remote(
-            merged_t.at[tile_rows(tile), :], odd_t.at[tile_rows(tile), :],
-            odd_send.at[tile], odd_recv.at[tile], beside,
-        )
-
-    def mate_copy(tile):
+    def odd_copy(piece):
+        rows = piece_rows(piece)
+        return remote(
+            merged_t.at[rows, :], odd_t.at[rows, :], odd_send.at[piece], odd_recv.at[piece], beside,
+        )
+
+    def mate_copy(piece):
+        rows = piece_rows(piece)
         return pltpu.make_async_remote_copy(
-            src_ref=pair_t.at[tile_rows(tile), :], dst_ref=pair_t.at[tile_rows(tile), :],
-            send_sem=mate_send.at[tile], recv_sem=mate_recv.at[tile],
+            src_ref=pair_t.at[rows, :], dst_ref=pair_t.at[rows, :],
+            send_sem=mate_send.at[piece], recv_sem=mate_recv.at[piece],
             device_id={"freq": mate, "sec": me}, device_id_type=MESH,
         )
-
-    own_pieces = modes // PIECE // 2 if shared else modes // PIECE
-    first_piece = (group % 2) * own_pieces if shared else 0
-    other_piece = own_pieces - first_piece
-
-    def piece_rows(piece):
-        return pl.ds(pl.multiple_of(piece * PIECE, PIECE), PIECE)
 
     def piece_copy(piece):
         rows = piece_rows(piece)
@@ -359,9 +360,7 @@
 
             each(batches, go)
 
-        @pl.when(section == 1)
-        def _():
-            each(tiles, lambda tile: tile_copy(tile).wait_recv())
+        each(tiles, lambda tile: tile_copy(tile).wait_recv())
 
         @pl.when(jnp.logical_and(section == 1, not_last))
         def _():
@@ -376,35 +375,37 @@
             each(batches, go)
 
         def merge_tile(tile):
-            rows = tile_rows(tile)
-
-            @pl.when(section != 1)
-            def _():
-                tile_copy(tile).wait_recv()
-
-            block = nn(upper_t[rows, :], lower_t[...]).astype(BF16)
-            merged[rows, :] = block
-            merged_t[:, rows] = block.T
-
-        each(tiles, merge_tile)
-
-        @pl.when(one_odd)
-        def _():
-            each(own_tiles, lambda place: odd_copy(first_own + place).start())
-
-        def pair_tile(place):
+            columns = tile_rows(tile)
+            block = nn(upper_t[...], lower_t[:, columns]).astype(BF16)
+            merged[:, columns] = block
+            merged_t[columns, :] = block.T
+
+        def own_merge(place):
             tile = first_own + place
-            rows = tile_rows(tile)
-            odd_copy(tile).wait_recv()
+            merge_tile(tile)
+
+            @pl.when(one_odd)
+            def _():
+                each(TILE // PIECE, lambda part: odd_copy(tile * (TILE // PIECE) + part).start())
+
+        each(own_tiles, own_merge)
+        if shared:
+            each(own_tiles, lambda place: merge_tile(first_other + place))
+
+        def pair_piece(place):
+            piece = first_piece + place
+            rows = piece_rows(piece)
+            odd_copy(piece).wait_recv()
             pair_t[rows, :] = nn(odd_t[rows, :], merged_t[...]).astype(BF16)
             if shared:
-                mate_copy(tile).start()
-
+                mate_copy(piece).start()
+
+        early_pieces = own_pieces // 2
         early = section >= 4
 
         @pl.when(jnp.logical_and(even_paired, early))
         def _():
-            pair_tile(0)
+            each(early_pieces, pair_piece)
 
         @pl.when(jnp.logical_and(on_one, is_turn))
         def _():
@@ -445,14 +446,14 @@
             def _():
                 @pl.when(jnp.logical_not(early))
                 def _():
-                    pair_tile(0)
-
-                each(own_tiles - 1, lambda place: pair_tile(place + 1))
+                    each(early_pieces, pair_piece)
+
+                each(own_pieces - early_pieces, lambda place: pair_piece(early_pieces + place))
                 each(batches, lambda batch: echo_copy(batch).wait_recv())
                 each(batches, lambda batch: odd_echo_copy(batch).wait_recv())
                 echo[...] += nn(odd_echo[...], merged_t[...])
                 if shared:
-                    each(own_tiles, lambda place: mate_copy(first_other + place).wait_recv())
+                    each(own_pieces, lambda place: mate_copy(other_piece + place).wait_recv())
 
             @pl.when(is_turn)
             def _():
@@ -519,12 +520,12 @@
 
             @pl.when(one_odd)
             def _():
-                each(own_tiles, lambda place: odd_copy(first_own + place).wait_send())
+                each(own_pieces, lambda place: odd_copy(first_piece + place).wait_send())
 
             if shared:
                 @pl.when(even_paired)
                 def _():
-                    each(own_tiles, lambda place: mate_copy(first_own + place).wait_send())
+                    each(own_pieces, lambda place: mate_copy(first_piece + place).wait_send())
 
                 @pl.when(is_turn)
                 def _():
@@ -565,16 +566,16 @@
             pltpu.VMEM((half, modes), BF16),
             pltpu.VMEM((count, modes), F32),
             pltpu.SemaphoreType.DMA((2,)),
-            tiles,
-            tiles,
-            per_batch,
-            per_batch,
-            pieces,
-            pieces,
-            pieces,
-            pieces,
-            tiles,
-            tiles,
+            pieces,
+            pieces,
+            per_batch,
+            per_batch,
+            pieces,
+            pieces,
+            pieces,
+            pieces,
+            pieces,
+            pieces,
             per_half,
             per_batch,
             tiles,

time: 46.9 us -> 47.1 us (level)
  no operation moved by 1% of the time
where the time goes in v7:
time: 47.1 us; the launch traced here: 47 us
  Pallas kernels  45.4 us (96%)
  local copies, waits for them, and re-layouts  1.57 us (3%)
    pallas_call x1, Pallas kernels, shards(): pl.pallas_call(functools.partial(kernel, n, groups), out_shape=jax.ShapeD...  45.4 us
    unnamed x1, local copies, waits for them, and re-layouts  1.57 us

profile of v7, /device:TPU:7, one launch (start us, length us, event | category | flops | bytes accessed | tf_op | source)
XLA Modules:
  0.0 47.0 jit_solution(8921949761995979266)
XLA Ops:
  0.0 45.4 %shard_map.37 = bf16[1,64,1024]{2,1,0:T(8,128)(2,1)} custom-call(s32[1,128]{1,0:T(1,128)} %bitcast.1, bf16[1,1024,1024]{2,1,0:T(8,128)(2,1)} %trans_ref.1, bf16[1,1024,1024]{2,1,0:T(8,128)(2,1)} %refl_ref.1), custom_call_target="tpu_custom_call" | custom-call | tf_op jit(solution)/shard_map/pallas_call | solution.py:554
  45.4 1.6 %copy.5 = bf16[1,64,1024]{2,1,0:T(8,128)(2,1)} copy(bf16[1,64,1024]{2,1,0:T(8,128)(2,1)} %shard_map.37) | data formatting | bytes 262144

commit v8 on v7

--- a/solution.py
+++ b/solution.py
@@ -362,18 +362,6 @@
 
         each(tiles, lambda tile: tile_copy(tile).wait_recv())
 
-        @pl.when(jnp.logical_and(section == 1, not_last))
-        def _():
-            def go(batch):
-                rows = batch_rows(batch)
-                down_copy(batch).wait_recv()
-                middle = nn(down_in[rows, :], upper_t[...]).astype(BF16)
-                down_out[rows, :] = nn(middle, lower_t[...]).astype(BF16)
-                down_copy(batch).start()
-                pass_copy(batch).start()
-
-            each(batches, go)
-
         def merge_tile(tile):
             columns = tile_rows(tile)
             block = nn(upper_t[...], lower_t[:, columns]).astype(BF16)
@@ -417,7 +405,7 @@
 
             each(own_pieces, swap)
 
-        @pl.when(jnp.logical_and(section > 1, not_last))
+        @pl.when(jnp.logical_and(not_first, not_last))
         def _():
             def go(batch):
                 rows = batch_rows(batch)
@@ -462,7 +450,9 @@
                 up_in[...] = nn(down_out[...], odd_t[...]).astype(BF16)
 
             def climb(step_t):
-                def go(batch):
+                def go(place):
+                    in_turn = (place % 2) * half_batches + place // 2
+                    batch = jnp.where(odd, in_turn, place)
                     rows = batch_rows(batch)
 
                     @pl.when(jnp.logical_not(even_paired))

time: 47.1 us -> 45.2 us (0.960)
  Pallas kernels: 45.4 us -> 43.5 us
    pallas_call x1, Pallas kernels: 45.4 us -> 43.5 us  [shards(): pl.pallas_call(functools.partial(kernel, n, groups), out_shape=jax.ShapeD...]
where the time goes in v8:
time: 45.2 us; the launch traced here: 45 us
  Pallas kernels  43.5 us (96%)
  local copies, waits for them, and re-layouts  1.57 us (3%)
    pallas_call x1, Pallas kernels, shards(): pl.pallas_call(functools.partial(kernel, n, groups), out_shape=jax.ShapeD...  43.5 us
    unnamed x1, local copies, waits for them, and re-layouts  1.57 us

profile of v8, /device:TPU:7, one launch (start us, length us, event | category | flops | bytes accessed | tf_op | source)
XLA Modules:
  0.0 45.0 jit_solution(7772951900947669764)
XLA Ops:
  0.0 43.5 %shard_map.37 = bf16[1,64,1024]{2,1,0:T(8,128)(2,1)} custom-call(s32[1,128]{1,0:T(1,128)} %bitcast.1, bf16[1,1024,1024]{2,1,0:T(8,128)(2,1)} %trans_ref.1, bf16[1,1024,1024]{2,1,0:T(8,128)(2,1)} %refl_ref.1), custom_call_target="tpu_custom_call" | custom-call | tf_op jit(solution)/shard_map/pallas_call | solution.py:544
  43.5 1.6 %copy.5 = bf16[1,64,1024]{2,1,0:T(8,128)(2,1)} copy(bf16[1,64,1024]{2,1,0:T(8,128)(2,1)} %shard_map.37) | data formatting | bytes 262144

commit v9 on v8

--- a/solution.py
+++ b/solution.py
@@ -7,7 +7,7 @@
 from jax.experimental.pallas import tpu as pltpu
 from jax.sharding import PartitionSpec as P
 
-ROWS = 32
+ROWS = 16
 TILE = 256
 PIECE = 128
 F32 = jnp.float32

time: 45.2 us -> 45.2 us (level)
  the two profiles are of different devices: /device:TPU:7 before, /device:TPU:5 now
where the time goes in v9:
time: 45.2 us; the launch traced here: 45 us
  Pallas kernels  43.4 us (96%)
  local copies, waits for them, and re-layouts  1.57 us (3%)
    pallas_call x1, Pallas kernels, shards(): pl.pallas_call(functools.partial(kernel, n, groups), out_shape=jax.ShapeD...  43.4 us
    unnamed x1, local copies, waits for them, and re-layouts  1.57 us

profile of v9, /device:TPU:5, one launch (start us, length us, event | category | flops | bytes accessed | tf_op | source)
XLA Modules:
  0.0 45.0 jit_solution(2290010453411743679)
XLA Ops:
  0.0 43.4 %shard_map.37 = bf16[1,64,1024]{2,1,0:T(8,128)(2,1)} custom-call(s32[1,128]{1,0:T(1,128)} %bitcast.1, bf16[1,1024,1024]{2,1,0:T(8,128)(2,1)} %trans_ref.1, bf16[1,1024,1024]{2,1,0:T(8,128)(2,1)} %refl_ref.1), custom_call_target="tpu_custom_call" | custom-call | tf_op jit(solution)/shard_map/pallas_call | solution.py:544
  43.5 1.6 %copy.5 = bf16[1,64,1024]{2,1,0:T(8,128)(2,1)} copy(bf16[1,64,1024]{2,1,0:T(8,128)(2,1)} %shard_map.37) | data formatting | bytes 262144

commit v10 on v9

--- a/solution.py
+++ b/solution.py
@@ -360,7 +360,16 @@
 
             each(batches, go)
 
-        each(tiles, lambda tile: tile_copy(tile).wait_recv())
+        quick = section <= 2
+
+        @pl.when(quick)
+        def _():
+            def row_tile(tile):
+                rows = tile_rows(tile)
+                tile_copy(tile).wait_recv()
+                merged[rows, :] = nn(upper_t[rows, :], lower_t[...]).astype(BF16)
+
+            each(tiles, row_tile)
 
         def merge_tile(tile):
             columns = tile_rows(tile)
@@ -376,9 +385,12 @@
             def _():
                 each(TILE // PIECE, lambda part: odd_copy(tile * (TILE // PIECE) + part).start())
 
-        each(own_tiles, own_merge)
-        if shared:
-            each(own_tiles, lambda place: merge_tile(first_other + place))
+        @pl.when(jnp.logical_not(quick))
+        def _():
+            each(tiles, lambda tile: tile_copy(tile).wait_recv())
+            each(own_tiles, own_merge)
+            if shared:
+                each(own_tiles, lambda place: merge_tile(first_other + place))
 
         def pair_piece(place):
             piece = first_piece + place
@@ -428,6 +440,25 @@
 
             each(batches, go)
 
+        @pl.when(quick)
+        def _():
+            def flip_tile(tile):
+                columns = tile_rows(tile)
+                merged_t[columns, :] = merged[:, columns].T
+
+                @pl.when(one_odd)
+                def _():
+                    each(TILE // PIECE, lambda part: flip_send(tile * (TILE // PIECE) + part))
+
+            def flip_send(piece):
+                mine = jnp.logical_and(piece >= first_piece, piece < first_piece + own_pieces)
+
+                @pl.when(mine)
+                def _():
+                    odd_copy(piece).start()
+
+            each(tiles, flip_tile)
+
         @pl.when(not_last)
         def _():
             @pl.when(even_paired)
@@ -450,9 +481,7 @@
                 up_in[...] = nn(down_out[...], odd_t[...]).astype(BF16)
 
             def climb(step_t):
-                def go(place):
-                    in_turn = (place % 2) * half_batches + place // 2
-                    batch = jnp.where(odd, in_turn, place)
+                def go(batch):
                     rows = batch_rows(batch)
 
                     @pl.when(jnp.logical_not(even_paired))
@@ -487,9 +516,21 @@
             def _():
                 climb(pair_t)
 
-            @pl.when(jnp.logical_not(even_paired))
+            @pl.when(is_turn)
             def _():
                 climb(merged_t)
+
+            @pl.when(one_odd)
+            def _():
+                for part in (0, 1):
+                    first = part * half_batches
+                    rows = slice(part * half, (part + 1) * half)
+                    each(half_batches, lambda place: echo_copy(first + place).wait_recv())
+                    each(half_batches, lambda place: up_copy(first + place).wait_recv())
+                    value = echo[rows, :] + nn(up_in[rows, :], merged_t[...])
+                    up_out[rows, :] = value.astype(BF16)
+                    if part == 0:
+                        each(half_batches, lambda place: half_copy(place).start())
 
             own_half()
             each(batches, lambda batch: down_copy(batch).wait_send())

time: 45.2 us -> 43.6 us (0.965)
  the two profiles are of different devices: /device:TPU:5 before, /device:TPU:7 now
where the time goes in v10:
time: 43.6 us; the launch traced here: 42.9 us
  Pallas kernels  41.3 us (95%)
  local copies, waits for them, and re-layouts  1.57 us (4%)
    pallas_call x1, Pallas kernels, shards(): pl.pallas_call(functools.partial(kernel, n, groups), out_shape=jax.ShapeD...  41.3 us
    unnamed x1, local copies, waits for them, and re-layouts  1.57 us

profile of v10, /device:TPU:7, one launch (start us, length us, event | category | flops | bytes accessed | tf_op | source)
XLA Modules:
  0.0 42.9 jit_solution(6506094893149551971)
XLA Ops:
  0.0 41.3 %shard_map.37 = bf16[1,64,1024]{2,1,0:T(8,128)(2,1)} custom-call(s32[1,128]{1,0:T(1,128)} %bitcast.1, bf16[1,1024,1024]{2,1,0:T(8,128)(2,1)} %trans_ref.1, bf16[1,1024,1024]{2,1,0:T(8,128)(2,1)} %refl_ref.1), custom_call_target="tpu_custom_call" | custom-call | tf_op jit(solution)/shard_map/pallas_call | solution.py:585
  41.3 1.6 %copy.5 = bf16[1,64,1024]{2,1,0:T(8,128)(2,1)} copy(bf16[1,64,1024]{2,1,0:T(8,128)(2,1)} %shard_map.37) | data formatting | bytes 262144

commit v11 on v10

--- a/solution.py
+++ b/solution.py
@@ -430,15 +430,11 @@
                 down_out[rows, :] = nn(down_in[rows, :], merged[...]).astype(BF16)
                 down_copy(batch).start()
 
-                @pl.when(paired)
-                def _():
-                    pass_copy(batch).start()
-
-                @pl.when(jnp.logical_and(odd, jnp.logical_not(paired)))
-                def _():
-                    pass_copy(batch).start()
-
             each(batches, go)
+
+            @pl.when(jnp.logical_not(is_turn))
+            def _():
+                each(batches, lambda batch: pass_copy(batch).start())
 
         @pl.when(quick)
         def _():

time: 43.6 us -> 44.3 us (1.016); the launches traced: 42.9 us -> 44.2 us
  Pallas kernels: 41.3 us -> 42.6 us
    pallas_call x1, Pallas kernels: 41.3 us -> 42.6 us  [shards(): pl.pallas_call(functools.partial(kernel, n, groups), out_shape=jax.ShapeD...]
where the time goes in v11:
time: 44.3 us; the launch traced here: 44.2 us
  Pallas kernels  42.6 us (96%)
  local copies, waits for them, and re-layouts  1.57 us (4%)
    pallas_call x1, Pallas kernels, shards(): pl.pallas_call(functools.partial(kernel, n, groups), out_shape=jax.ShapeD...  42.6 us
    unnamed x1, local copies, waits for them, and re-layouts  1.57 us

profile of v11, /device:TPU:7, one launch (start us, length us, event | category | flops | bytes accessed | tf_op | source)
XLA Modules:
  0.0 44.2 jit_solution(4989701936573548464)
XLA Ops:
  0.0 42.6 %shard_map.37 = bf16[1,64,1024]{2,1,0:T(8,128)(2,1)} custom-call(s32[1,128]{1,0:T(1,128)} %bitcast.1, bf16[1,1024,1024]{2,1,0:T(8,128)(2,1)} %trans_ref.1, bf16[1,1024,1024]{2,1,0:T(8,128)(2,1)} %refl_ref.1), custom_call_target="tpu_custom_call" | custom-call | tf_op jit(solution)/shard_map/pallas_call | solution.py:581
  42.6 1.6 %copy.5 = bf16[1,64,1024]{2,1,0:T(8,128)(2,1)} copy(bf16[1,64,1024]{2,1,0:T(8,128)(2,1)} %shard_map.37) | data formatting | bytes 262144
